TPU v7x, 32 devices: a whole 2x2x4 slice. The times are simulated.
32 devices in a mesh: groups: 2 (over x), agent: 8 (over z, y), tm: 2 (over core).
Axes of the slice: x: 2, y: 2, z: 4, core: 2. Of those that a mesh axis runs over, the one named last changes fastest.
Arguments:
- embedded: bfloat16 [64, 1024, 512], P(('groups', 'tm'), 'agent'), parts along dimension 0, may hold values from -6 to 6
- block_lists: int32 [16, 32, 2], P(('groups', 'agent'), 'tm'), parts along dimension 0, may hold values from 0 to 7, all different within a row; in each aligned block of 16 rows (0 to 15, 16 to 31, ..., all dimensions but the last counted through in order) at most 8 rows name the same one
- done_flags: int32 [64, 1024], P(('groups', 'tm'), 'agent'), parts along dimension 0, may hold values 0 or 1
- rewards: float32 [64, 1024], P(('groups', 'tm'), 'agent'), parts along dimension 0, may hold values from -1.2 to 1.2
- bootstrap: float32 [2048], P(('groups', 'agent')), parts along dimension 0, may hold values from -6 to 6
- agent_proj: bfloat16 [512, 1536], replicated, may hold values from -2 to 2
- agent_merge: bfloat16 [512, 512], replicated, may hold values from -0.75 to 0.75
- time_proj: bfloat16 [512, 1536], replicated, may hold values from -2 to 2
- time_merge: bfloat16 [512, 512], replicated, may hold values from -0.75 to 0.75
- value_weight: float32 [512], replicated, may hold values from -0.25 to 0.25
Outputs:
- values: float32 [64, 1024], P(('groups', 'tm'), 'agent'), parts along dimension 0
- advantages: float32 [64, 1024], P(('groups', 'tm'), 'agent'), parts along dimension 0
There are 2 independent parts, one for each index of `groups`. A program takes and returns all parts, laid end to end along the dimension named above; an argument that names none is the same for every part. Nothing has to cross between parts.
Inputs may be any that keep to these rules, and one draw needn't show every extreme that they name: `block_lists`: each row names 2 different agent blocks. Within the 16 rows of one block along the second dimension no agent block is named more than 8 times, and some agent block is named exactly 8 times.
All inputs are finite; a program needn't handle non-finite values. No bound on the sum of `done_flags` on one device may be relied on, other than what follows from the above.
Results may differ from a plain program's by a relative error of at most 0.0085.
Values may be sent and summed in bfloat16 or wider, within the bound.
No kernel may reach another device: no remote copies, remote signals or barrier semaphores. Data moves between devices by JAX's collectives and lax.ppermute only.
A program may use at most 128 MiB of HBM per device.

v0:
```python
import functools
import math

import jax
import jax.numpy as jnp
from jax import lax
from jax.experimental import pallas as pl
from jax.experimental.pallas import tpu as pltpu
from jax.sharding import PartitionSpec as P

HEADS = 8
WINDOW = 16
discount = 0.9997
trace_decay = 0.995
epsilon = 1e-06
bf16 = jnp.bfloat16
f32 = jnp.float32
MIB = 1024 * 1024
SPAN = 1024
COLUMNS = 4
ROWS = 2


def rms(values):
    return values * lax.rsqrt(jnp.mean(values * values, axis=-1, keepdims=True) + epsilon)


def dot(a, b):
    return jnp.dot(a, b, preferred_element_type=f32)


def dot_t(a, b):
    return lax.dot_general(a, b, (((1,), (1,)), ((), ())), preferred_element_type=f32)


def attend(queries, keys, values, head_size, bias):
    rows, width = queries.shape
    scale = head_size ** (-0.5) * math.log2(math.e)
    pair = 2 * head_size
    lane = lax.broadcasted_iota(jnp.int32, (rows, pair), 1)
    first = lane < head_size
    ones = jnp.ones((keys.shape[0], pair), bf16)
    mixed = []
    for at in range(0, width, pair):
        both = queries[:, at : at + pair]
        none = jnp.zeros_like(both)
        stacked = jnp.concatenate(
            [jnp.where(first, both, none), jnp.where(first, none, both)], axis=0
        )
        scores = dot_t(stacked, keys[:, at : at + pair])
        if bias is not None:
            scores = scores + bias
        weights = jnp.exp2((scores - jnp.max(scores, axis=-1, keepdims=True)) * scale).astype(bf16)
        summed = dot(weights, jnp.concatenate([values[:, at : at + pair], ones], axis=1))
        result = summed[:, :pair] / summed[:, pair:]
        mixed.append(jnp.where(first, result[:rows], result[rows:]).astype(bf16))
    return jnp.concatenate(mixed, axis=1)


def fetch(entry, arrays, target, sem):
    for code, ref in arrays.items():

        @pl.when(entry // SPAN == code)
        def _(ref=ref):
            pltpu.make_async_copy(ref.at[entry % SPAN], target, sem).start()


def own_kernel(idle, own_ref, proj_ref, *refs):
    projected_ref = refs[idle]
    together, agents, width = own_ref.shape
    mine = rms(own_ref[...].astype(f32).reshape(together * agents, width)).astype(bf16)
    projected = dot(mine, proj_ref[...]).astype(bf16)
    projected_ref[...] = projected.reshape(together, agents, proj_ref.shape[1])


def own_stage(embedded, proj, after=()):
    steps, agents, width = embedded.shape
    together = math.gcd(steps, 4)
    return pl.pallas_call(
        functools.partial(own_kernel, len(after)),
        grid=(steps // together,),
        in_specs=[
            pl.BlockSpec((together, agents, width), lambda i: (i, 0, 0)),
            pl.BlockSpec(proj.shape, lambda i: (0, 0)),
        ]
        + [pl.BlockSpec(memory_space=pltpu.HBM)] * len(after),
        out_specs=pl.BlockSpec((together, agents, proj.shape[1]), lambda i: (i, 0, 0)),
        out_shape=jax.ShapeDtypeStruct((steps, agents, proj.shape[1]), bf16),
        compiler_params=pltpu.CompilerParams(vmem_limit_bytes=20 * MIB),
        name="own_stage",
    )(embedded, proj, *after)


def agent_kernel(
    list_length, first_step, codes, idle, head_size, table_ref, own_ref, projected_ref, *refs
):
    arrays = dict(zip(codes, refs))
    proj_ref, merge_ref, residual_ref, normed_ref, held_ref, sems = refs[len(codes) + idle :]
    together, agents, width = own_ref.shape
    turn = pl.program_id(0)
    pieces = [(s, j) for s in range(together) for j in range(list_length)]

    def begin(turn):
        slot = turn % 2
        for n, (s, j) in enumerate(pieces):
            entry = table_ref[(first_step + turn * together + s) * list_length + j]
            fetch(entry, arrays, held_ref.at[slot, n], sems.at[slot, n])

    @pl.when(turn == 0)
    def _():
        begin(turn)

    @pl.when(turn + 1 < pl.num_programs(0))
    def _():
        begin(turn + 1)

    slot = turn % 2
    for n in range(len(pieces)):
        pltpu.make_async_copy(refs[0].at[0], held_ref.at[slot, n], sems.at[slot, n]).wait()
    own = own_ref[...].astype(f32).reshape(together * agents, width)
    listed = held_ref[slot].astype(f32).reshape(len(pieces) * agents, width)
    theirs = rms(listed).astype(bf16)
    projected = projected_ref[...].reshape(together * agents, 3 * width)
    queries, near = projected[:, :width], projected[:, width:]
    away = dot(theirs, proj_ref[:, width:]).astype(bf16)
    mixed = []
    for s in range(together):
        here = slice(s * agents, (s + 1) * agents)
        there = slice(s * list_length * agents, (s + 1) * list_length * agents)
        keyvals = jnp.concatenate([near[here], away[there]], axis=0)
        mixed.append(
            attend(queries[here], keyvals[:, :width], keyvals[:, width:], head_size, None)
        )
    residual = own + dot(jnp.concatenate(mixed, axis=0), merge_ref[...])
    residual_ref[...] = residual.reshape(together, agents, width)
    normed_ref[...] = rms(residual).astype(bf16).reshape(together, agents, width)


def agent_stage(
    embedded, projected, arrays, table, first_step, steps, list_length, proj, merge, after=()
):
    _, agents, width = embedded.shape
    together = math.gcd(steps, math.gcd(first_step, 2))
    piece = (together, agents, width)
    whole = lambda i, w: (0, 0)
    flops = 2 * steps * agents * width * width * (4 + 2 * list_length + 2 * (1 + list_length))
    return pl.pallas_call(
        functools.partial(
            agent_kernel, list_length, first_step, tuple(arrays), len(after), width // HEADS
        ),
        grid_spec=pltpu.PrefetchScalarGridSpec(
            num_scalar_prefetch=1,
            grid=(steps // together,),
            in_specs=[
                pl.BlockSpec((together, agents, cols), lambda i, w: (first_step // together + i, 0, 0))
                for cols in (width, 3 * width)
            ]
            + [pl.BlockSpec(memory_space=pltpu.HBM)] * (len(arrays) + len(after))
            + [pl.BlockSpec(proj.shape, whole), pl.BlockSpec(merge.shape, whole)],
            out_specs=[pl.BlockSpec(piece, lambda i, w: (i, 0, 0))] * 2,
            scratch_shapes=[
                pltpu.VMEM((2, together * list_length, agents, width), bf16),
                pltpu.SemaphoreType.DMA((2, together * list_length)),
            ],
        ),
        out_shape=[
            jax.ShapeDtypeStruct((steps, agents, width), f32),
            jax.ShapeDtypeStruct((steps, agents, width), bf16),
        ],
        compiler_params=pltpu.CompilerParams(vmem_limit_bytes=24 * MIB),
        cost_estimate=pl.CostEstimate(
            flops=5 * flops, bytes_accessed=steps * agents * width * 12, transcendentals=0
        ),
        name="agent_stage",
    )(table, embedded, projected, *arrays.values(), *after, proj, merge)


def pack_kernel(codes, parts, idle, flagged, table_ref, *refs):
    arrays = dict(zip(codes, refs))
    outs, (held_ref, in_sems, out_sems) = refs[len(codes) + idle : -3], refs[-3:]
    if flagged:
        outs[-1][...] = jnp.full(outs[-1].shape, outs[0][0], jnp.int32)
        outs = outs[1:-1]
    slots = []
    for out, (offset, count, first) in zip(outs, parts):
        slots += [(offset, first, n, out.at[n]) for n in range(count)]

    def guarded(offset, n, action):
        if offset is None:
            action()
        else:
            pl.when(table_ref[offset + n] >= 0)(action)

    for at, (offset, first, n, _) in enumerate(slots):
        if offset is None:
            own = arrays[0].at[first + n]
            pltpu.make_async_copy(own, held_ref.at[at], in_sems.at[at]).start()
        else:
            fetch(table_ref[offset + n], arrays, held_ref.at[at], in_sems.at[at])
    for at, (offset, first, n, target) in enumerate(slots):

        def pass_on(at=at, target=target):
            pltpu.make_async_copy(refs[0].at[0], held_ref.at[at], in_sems.at[at]).wait()
            pltpu.make_async_copy(held_ref.at[at], target, out_sems.at[at]).start()

        guarded(offset, n, pass_on)
    for at, (offset, first, n, target) in enumerate(slots):

        def finish(at=at, target=target):
            pltpu.make_async_copy(held_ref.at[at], target, out_sems.at[at]).wait()

        guarded(offset, n, finish)


def pack(table, arrays, parts, after=(), flag=None):
    piece = next(iter(arrays.values())).shape[1:]
    slots = sum(count for _, count, _ in parts)
    smem = pl.BlockSpec(memory_space=pltpu.SMEM)
    hbm = pl.BlockSpec(memory_space=pltpu.HBM)
    flags = () if flag is None else (flag,)
    out_specs = [hbm] * len(parts)
    out_shape = [jax.ShapeDtypeStruct((count,) + piece, bf16) for _, count, _ in parts]
    if flags:
        out_specs.append(pl.BlockSpec(memory_space=pltpu.VMEM))
        out_shape.append(jax.ShapeDtypeStruct((8, 128), jnp.int32))
    return pl.pallas_call(
        functools.partial(pack_kernel, tuple(arrays), tuple(parts), len(after), len(flags)),
        in_specs=[smem] + [hbm] * (len(arrays) + len(after)) + [smem] * len(flags),
        out_specs=out_specs,
        out_shape=out_shape,
        scratch_shapes=[
            pltpu.VMEM((slots,) + piece, bf16),
            pltpu.SemaphoreType.DMA((slots,)),
            pltpu.SemaphoreType.DMA((slots,)),
        ],
        cost_estimate=pl.CostEstimate(
            flops=0, bytes_accessed=piece[0] * piece[1], transcendentals=0
        ),
        compiler_params=pltpu.CompilerParams(
            vmem_limit_bytes=slots * piece[0] * piece[1] * 2 + 2 * MIB
        ),
        name="pack",
    )(table, *arrays.values(), *after, *flags)


def suffix(values, rewards, done, next_value, next_advantage):
    steps = values.shape[0]
    living = 1.0 - done.astype(f32)
    running, following, rows = next_advantage, next_value, [None] * steps
    for step in range(steps - 1, -1, -1):
        alive = living[step : step + 1]
        value = values[step : step + 1]
        change = rewards[step : step + 1] + discount * alive * following - value
        running = change + discount * trace_decay * alive * running
        rows[step] = running
        following = value
    return rows


def time_kernel(parts, steps, tile, head_size, offset_ref, *refs):
    refs = list(refs)
    residual_refs = [refs.pop(0) for _ in range(parts)]
    rim_refs = [refs.pop(0) for _ in range(parts)]
    proj_ref, merge_ref, weight_ref, done_ref, rewards_ref, boot_ref = refs[:6]
    values_ref, edge_ref, bias_ref = refs[6:]
    width = proj_ref.shape[0]
    turn = pl.program_id(0)
    group = 8
    rows = steps * group
    agents = values_ref.shape[1]

    @pl.when(turn == 0)
    def _():
        r = lax.broadcasted_iota(jnp.int32, (2 * rows, 2 * rows), 0) % rows
        c = lax.broadcasted_iota(jnp.int32, (2 * rows, 2 * rows), 1)
        query_step = r // group
        key_step = c // group - steps
        allowed = (
            (r % group == c % group)
            & (key_step <= query_step)
            & (key_step > query_step - WINDOW)
            & (key_step + offset_ref[0] >= 0)
        )
        bias_ref[...] = jnp.where(allowed, 0.0, -1e30)
        values_ref[...] = jnp.zeros_like(values_ref)

    def pieces(part_refs):
        whole = jnp.concatenate([ref[...].astype(f32) for ref in part_refs], axis=0)
        return [
            whole[:, at : at + group].reshape(rows, width) for at in range(0, tile, group)
        ]

    residuals = pieces(residual_refs)
    current = jnp.concatenate([rms(r).astype(bf16) for r in residuals], axis=0)
    behind = jnp.concatenate([r.astype(bf16) for r in pieces(rim_refs)], axis=0)
    projected = dot(current, proj_ref[...]).astype(bf16)
    before = dot(behind, proj_ref[:, width:]).astype(bf16)
    bias = bias_ref[...]
    mixed = []
    for at in range(0, tile * steps, rows):
        mine, past = projected[at : at + rows], before[at : at + rows]
        keys = jnp.concatenate([past[:, :width], mine[:, width : 2 * width]], axis=0)
        held = jnp.concatenate([past[:, width:], mine[:, 2 * width :]], axis=0)
        mixed.append(attend(mine[:, :width], keys, held, head_size, bias))
    merged = dot(jnp.concatenate(mixed, axis=0), merge_ref[...])
    lane = lax.broadcasted_iota(jnp.int32, (steps, group, agents), 2)
    place = lax.broadcasted_iota(jnp.int32, (steps, group, agents), 1)
    total = values_ref[...]
    for n, residual in enumerate(residuals):
        final = rms(residual + merged[n * rows : (n + 1) * rows])
        value = jnp.sum(final * weight_ref[...], axis=-1, keepdims=True)
        spot = lane == place + (turn * tile + n * group)
        total = total + jnp.sum(
            jnp.where(spot, value.reshape(steps, group, 1), 0.0), axis=1
        )
    values_ref[...] = total

    @pl.when(turn == pl.num_programs(0) - 1)
    def _():
        found = values_ref[...]
        boot = boot_ref[...]
        advantages = suffix(found, rewards_ref[...], done_ref[...], boot, jnp.zeros_like(boot))
        edge_ref[...] = jnp.concatenate([found[:1], advantages[0]], axis=0)


def time_stage(residuals, rims, offset, proj, merge, weight, done, rewards, boot):
    part_steps = [r.shape[0] for r in residuals]
    steps = sum(part_steps)
    _, agents, width = residuals[0].shape
    tile = math.gcd(agents, 32)
    whole = lambda i, o: (0, 0)

    def blocks(arrays):
        return [
            pl.BlockSpec((array.shape[0], tile, width), lambda i, o: (0, i, 0))
            for array in arrays
        ]

    rows = 16 * steps
    fixed = [proj, merge, weight, done, rewards, boot]
    return pl.pallas_call(
        functools.partial(time_kernel, len(residuals), steps, tile, width // HEADS),
        grid_spec=pltpu.PrefetchScalarGridSpec(
            num_scalar_prefetch=1,
            grid=(agents // tile,),
            in_specs=blocks(residuals)
            + blocks(rims)
            + [pl.BlockSpec(array.shape, whole) for array in fixed],
            out_specs=[
                pl.BlockSpec((steps, agents), whole),
                pl.BlockSpec((2, agents), whole),
            ],
            scratch_shapes=[pltpu.VMEM((rows, rows), f32)],
        ),
        out_shape=[
            jax.ShapeDtypeStruct((steps, agents), f32),
            jax.ShapeDtypeStruct((2, agents), f32),
        ],
        compiler_params=pltpu.CompilerParams(vmem_limit_bytes=28 * MIB),
        cost_estimate=pl.CostEstimate(flops=0, bytes_accessed=rows, transcendentals=0),
        name="time_stage",
    )(offset, *residuals, *rims, *fixed)


def advantage_kernel(last_ref, values_ref, rewards_ref, done_ref, boot_ref, edge_ref, out_ref, mine_ref):
    last = last_ref[0] > 0
    arriving = edge_ref[...]
    boot = boot_ref[...]
    found = values_ref[...]
    next_value = jnp.where(last, boot, arriving[:1])
    next_advantage = jnp.where(last, 0.0, arriving[1:2])
    rows = suffix(found, rewards_ref[...], done_ref[...], next_value, next_advantage)
    out_ref[...] = jnp.concatenate(rows, axis=0)
    mine_ref[...] = jnp.concatenate([found[:1], rows[0]], axis=0)


def advantage_stage(last, values, rewards, done, boot, edge):
    return pl.pallas_call(
        advantage_kernel,
        in_specs=[pl.BlockSpec(memory_space=pltpu.SMEM)]
        + [pl.BlockSpec(memory_space=pltpu.VMEM)] * 5,
        out_specs=[pl.BlockSpec(memory_space=pltpu.VMEM)] * 2,
        out_shape=[
            jax.ShapeDtypeStruct(values.shape, f32),
            jax.ShapeDtypeStruct(edge.shape, f32),
        ],
        name="advantage_stage",
    )(last, values, rewards, done, boot, edge)


def exchange_slots(embedded, lists, capacity):
    steps, agents, width = embedded.shape
    blocks = lax.axis_size("agent")
    list_length = lists.shape[1]
    named = lists.reshape(-1)
    row_steps = jnp.arange(named.shape[0], dtype=jnp.int32) // list_length
    hits = (named[:, None] == jnp.arange(blocks, dtype=jnp.int32)[None, :]).astype(jnp.int32)
    slot = jnp.sum((jnp.cumsum(hits, axis=0) - hits) * hits, axis=1)
    slot_hits = (slot[:, None] == jnp.arange(capacity, dtype=jnp.int32)[None, :]).astype(jnp.int32)
    requests = jnp.sum(
        (hits * row_steps[:, None])[:, :, None] * slot_hits[:, None, :], axis=0
    )
    wanted = lax.all_to_all(requests, "agent", split_axis=0, concat_axis=0, tiled=True)
    outgoing = embedded[wanted.reshape(-1)].reshape(blocks, capacity, agents, width)
    arrived = lax.all_to_all(outgoing, "agent", split_axis=0, concat_axis=0, tiled=True)
    return arrived.reshape(blocks * capacity, agents, width), named * capacity + slot


OUTWARD_READY = {1: (0, 1, 1), 2: (1, 3, 3), 3: (2, 3, 4)}
ACROSS_READY = {0: (1, 2, 2), 1: (0, 0, 0), 2: (1, 3, 3), 3: (2, 3, 4)}
OUTWARD_DUE = (3, 4, 4)
ACROSS_DUE = (3, 4, 5)


def relay_sizes(steps, capacity):
    half, quarter = steps // 2, steps // 4
    chunks = [half, quarter, quarter]
    outward = [half, half, half, half, quarter + 2]
    across = [quarter, half, half, half - 1, quarter + 2, quarter + 2]
    return chunks, outward, across


def relay_codes(outward, across):
    names = {}
    code = 1
    for name, count in (("edge", len(outward)), ("swap", 2), ("far", 3), ("across", len(across))):
        names[name] = [code + n for n in range(count)]
        code += count
    names["own"] = 0
    return names


def inner_place(codes, starts, u, k):
    behind = starts[k] - starts[min(k, 1)]
    if u == 0:
        return codes["edge"][min(k, 1)] * SPAN + behind
    if u == 1:
        return codes["own"] * SPAN + starts[k]
    if u == 2:
        return codes["swap"][min(k, 1)] * SPAN + behind
    return codes["far"][k] * SPAN


def plan_kernel(steps, list_length, chunks, outward, across, place_ref, lists_ref, out_ref, in_ref, flag_ref, eloc, yloc, room):
    codes = relay_codes(outward, across)
    column, row = place_ref[0], place_ref[1]
    far_side = column >= COLUMNS // 2
    mirror = lambda u: jnp.where(far_side, COLUMNS - 1 - u, u)
    me = mirror(column)
    inner = me == 1
    starts = [sum(chunks[:k]) for k in range(len(chunks))]
    e_base = [sum(outward[:b]) for b in range(len(outward))]
    y_base = [sum(outward) + sum(across[:b]) for b in range(len(across))]
    block = lambda c, r: c * ROWS + r
    entry = lambda c, r, t, j: lists_ref[((c * ROWS + r) * steps + t) * list_length + j]

    def clear(n, _):
        out_ref[n] = -1
        return 0

    lax.fori_loop(0, sum(outward) + sum(across), clear, 0)

    @pl.when(me == 0)
    def _():
        for n in range(outward[1]):
            out_ref[e_base[1] + n] = codes["own"] * SPAN + starts[1] + n

    def named(place, r, t, source):
        hit = entry(place, r, t, 0) == source
        for j in range(1, list_length):
            hit = hit | (entry(place, r, t, j) == source)
        return hit

    def choose(sizes, ready):
        batch = jnp.int32(-1)
        for b in range(len(sizes) - 1, -1, -1):
            batch = jnp.where((room[b] < sizes[b]) & (b >= ready), b, batch)
        return batch

    def base_of(bases, batch):
        base = jnp.int32(0)
        for b, value in enumerate(bases):
            base = jnp.where(batch == b, value, base)
        return base

    def empty(sizes):
        for b in range(len(sizes)):
            room[b] = 0

    for turn in range(2):
        sender = row if turn == 0 else 1 - row
        empty(outward)
        room[0] = outward[0]
        for k, count in enumerate(chunks):
            for u in (1, 2, 3):

                def first_piece(n, _):
                    eloc[(turn * COLUMNS + 1) * steps + n] = n
                    return 0

                if u == 1 and k == 0:
                    lax.fori_loop(0, count, first_piece, 0)
                    continue

                def outer_piece(n, _, u=u, k=k):
                    t = starts[k] + n
                    source = block(mirror(u), sender)
                    need = named(0, 0, t, source)
                    for r in range(1, ROWS):
                        need = need | named(0, r, t, source)
                    batch = choose(outward, OUTWARD_READY[u][k])
                    eloc[(turn * COLUMNS + u) * steps + t] = -1

                    @pl.when(need & (batch >= 0))
                    def _():
                        slot = room[batch]
                        room[batch] = slot + 1
                        eloc[(turn * COLUMNS + u) * steps + t] = batch * SPAN + slot
                        if turn == 0:

                            @pl.when(inner)
                            def _():
                                out_ref[base_of(e_base, batch) + slot] = inner_place(codes, starts, u, k) + n

                    return 0

                lax.fori_loop(0, count, outer_piece, 0)

    for turn in range(2):
        sender = row if turn == 0 else 1 - row
        empty(across)
        for k, count in enumerate(chunks):
            for u in range(COLUMNS):

                def row_piece(n, _, u=u, k=k):
                    t = starts[k] + n
                    need = named(me, 1 - sender, t, block(mirror(u), sender))
                    if u == 0:
                        lies = jnp.int32(codes["own"] * SPAN) + t
                        when = jnp.int32(0)
                    else:
                        where = eloc[(turn * COLUMNS + u) * steps + t]
                        lies = codes["edge"][0] * SPAN + where
                        when = jnp.where(where < 0, len(across), where // SPAN + 1)
                    when = jnp.where(inner, ACROSS_READY[u][k], when)
                    lies = jnp.where(inner, inner_place(codes, starts, u, k) + n, lies)
                    batch = choose(across, when)
                    yloc[(turn * COLUMNS + u) * steps + t] = -1

                    @pl.when(need & (batch >= 0))
                    def _():
                        slot = room[batch]
                        room[batch] = slot + 1
                        yloc[(turn * COLUMNS + u) * steps + t] = batch * SPAN + slot
                        if turn == 0:
                            out_ref[base_of(y_base, batch) + slot] = lies

                    return 0

                lax.fori_loop(0, count, row_piece, 0)

    flag_ref[0] = 0
    for k, count in enumerate(chunks):

        def listed_piece(n, _, k=k):
            t = starts[k] + n // list_length
            source = entry(me, row, t, n % list_length)
            u = mirror(source // ROWS)
            same = source % ROWS == row
            e = eloc[u * steps + t]
            y = yloc[(COLUMNS + u) * steps + t]
            first = jnp.int32(0)
            for w in (0, 2, 3):
                first = jnp.where(u == w, inner_place(codes, starts, w, k), first)
            direct = jnp.where(inner, first + t - starts[k], codes["edge"][0] * SPAN + e)
            direct = jnp.where(u == me, codes["own"] * SPAN + t, direct)
            local = inner | (u == me)
            bad = jnp.where(
                same,
                jnp.logical_not(local) & ((e < 0) | (e // SPAN > OUTWARD_DUE[k])),
                (y < 0) | (y // SPAN > ACROSS_DUE[k]),
            )
            place = jnp.where(same, direct, codes["across"][0] * SPAN + y)
            in_ref[t * list_length + n % list_length] = jnp.where(bad, codes["own"] * SPAN, place)

            @pl.when(bad)
            def _():
                flag_ref[0] = 1

            return 0

        lax.fori_loop(0, count * list_length, listed_piece, 0)


def plan(lists_near, place, steps, list_length, chunks, outward, across):
    smem = pl.BlockSpec(memory_space=pltpu.SMEM)
    slots = sum(outward) + sum(across)
    return pl.pallas_call(
        functools.partial(plan_kernel, steps, list_length, chunks, outward, across),
        in_specs=[smem, smem],
        out_specs=[smem] * 3,
        out_shape=[
            jax.ShapeDtypeStruct((slots,), jnp.int32),
            jax.ShapeDtypeStruct((steps * list_length,), jnp.int32),
            jax.ShapeDtypeStruct((1,), jnp.int32),
        ],
        scratch_shapes=[
            pltpu.SMEM((2 * COLUMNS * steps,), jnp.int32),
            pltpu.SMEM((2 * COLUMNS * steps,), jnp.int32),
            pltpu.SMEM((max(len(outward), len(across)),), jnp.int32),
        ],
        name="plan",
    )(place, lists_near)


def shared(value, axes):
    count = lax.axis_size(axes)
    rows = jnp.broadcast_to(value[None], (count,) + value.shape)
    return lax.all_to_all(rows, axes, split_axis=0, concat_axis=0, tiled=True)


def column_pairs(moves):
    return [(a * ROWS + r, b * ROWS + r) for a, b in moves for r in range(ROWS)]


def relay(embedded, lists, capacity, attention, own_projection):
    steps, agents, width = embedded.shape
    list_length = lists.shape[1]
    chunks, outward, across = relay_sizes(steps, capacity)
    codes = relay_codes(outward, across)
    starts = [sum(chunks[:k]) for k in range(len(chunks))]
    e_base = [sum(outward[:b]) for b in range(len(outward))]
    y_base = [sum(outward) + sum(across[:b]) for b in range(len(across))]
    index = lax.axis_index("agent")
    place = jnp.stack([index // ROWS, index % ROWS]).astype(jnp.int32)
    send = lambda value, pairs: lax.ppermute(value, "agent", pairs)
    edges = column_pairs([(0, 1), (1, 0), (2, 3), (3, 2)])
    swap = column_pairs([(1, 2), (2, 1)])
    over = [(c * ROWS + r, c * ROWS + 1 - r) for c in range(COLUMNS) for r in range(ROWS)]
    own, edge, swapped, far, rows = (codes[n] for n in ("own", "edge", "swap", "far", "across"))
    arrays = {own: embedded}

    def pick(names):
        return {code: arrays[code] for code in names}

    def across_part(n):
        return (y_base[n], across[n], None)

    def stage(n, reads, settled, after=(), flag=None):
        parts = [across_part(n)]
        if n < len(outward):
            parts.append((e_base[n], outward[n], None))
        if n == 1:
            parts.append((None, outward[1], starts[1]))
        after = tuple(arrays[rows[b]] for b in settled) + tuple(after)
        packed = pack(out_table, pick([own] + reads), parts, after, flag)
        if n < len(outward):
            arrays[edge[n]] = send(packed[1], edges)
        arrays[rows[n]] = send(packed[0], over)
        return packed

    mine = lists.reshape(-1)
    beside = send(mine, over)
    pair = jnp.stack([jnp.where(index % ROWS == r, mine, beside) for r in range(ROWS)])
    inward = column_pairs([(0, 1), (COLUMNS - 1, COLUMNS - 2)])
    outer_pair = send(pair, inward)
    column = index // ROWS
    outer = (column == 0) | (column == COLUMNS - 1)
    near = jnp.concatenate([jnp.where(outer, pair, outer_pair), pair], axis=0).reshape(-1)
    begin = jnp.minimum(near[0], 0)
    first = lax.dynamic_slice_in_dim(embedded, begin, chunks[0], 0)
    arrays[edge[0]] = send(first, edges)
    arrays[swapped[0]] = send(first, swap)
    out_table, in_table, flag = plan(
        near, place, steps, list_length, chunks, outward, across
    )
    (token,) = pack(out_table, pick([own]), [across_part(0)])
    arrays[rows[0]] = send(token, over)
    arrays[far[0]] = send(arrays[edge[0]], swap)
    reads = edge[:1] + swapped[:1]
    packed = stage(1, reads, (0,), (token,))
    arrays[swapped[1]] = send(packed[2], swap)
    for k in (1, 2):
        at = starts[k] - starts[1]
        arrays[far[k]] = send(arrays[edge[1]][at : at + chunks[k]], swap)
    reads = reads + edge[1:2] + far[:1]
    projected = own_projection(packed[:1])
    packed = stage(2, reads, (1,), (projected,))
    reads = reads + edge[2:3] + swapped[1:] + far[1:2]
    packed = stage(3, reads, (2,), packed[:1])
    reads = reads + edge[3:4] + far[2:3]
    packed = stage(4, reads, (3,), packed[:1])

    def attend_chunk(k, after):
        return attention(
            starts[k], chunks[k], due(arrays, codes, starts, k), in_table, projected, after
        )

    done = [attend_chunk(0, packed[:1])]
    reads = reads + edge[4:5]
    packed = stage(5, reads, (4,), (done[0][0],), flag)
    done.append(attend_chunk(1, packed[:1]))
    crowded = jnp.max(lax.all_gather(packed[-1], ("groups", "agent", "tm")))
    done.append(attend_chunk(2, (done[1][0],)))
    return done, crowded


def due(arrays, codes, starts, k):
    wanted = {codes["own"], *codes["edge"][: OUTWARD_DUE[k] + 1]}
    wanted |= {inner_place(codes, starts, u, k) // SPAN for u in (0, 2, 3)}
    wanted |= set(codes["across"][: ACROSS_DUE[k] + 1])
    return {code: arrays[code] for code in sorted(wanted)}


def body(
    embedded,
    block_lists,
    done_flags,
    rewards,
    bootstrap,
    agent_proj,
    agent_merge,
    time_proj,
    time_merge,
    value_weight,
):
    steps, agents, width = embedded.shape
    list_length = block_lists.shape[2]
    blocks = lax.axis_size("agent")
    lists = block_lists[0]
    capacity = max(2, (2 * steps * list_length + blocks - 1) // blocks)
    spans = lax.axis_size("tm")
    index = lax.axis_index("tm")
    offset = (index * steps).astype(jnp.int32).reshape(1)
    boot = bootstrap.reshape(1, agents)
    forward = [(i, i + 1) for i in range(spans - 1)]
    backward = [(i + 1, i) for i in range(spans - 1)]

    def own_projection(after=()):
        return own_stage(embedded, agent_proj, after)

    def attention(first, count, arrays, table, projected, after=()):
        residual, normed = agent_stage(
            embedded,
            projected,
            arrays,
            table,
            first,
            count,
            list_length,
            agent_proj,
            agent_merge,
            after,
        )
        return residual, lax.ppermute(normed, "tm", forward)

    def finish(done):
        residuals, rims = [part[0] for part in done], [part[1] for part in done]
        values, edge = time_stage(
            residuals,
            rims,
            offset,
            time_proj,
            time_merge,
            value_weight.reshape(1, width),
            done_flags,
            rewards,
            boot,
        )
        last = (index == spans - 1).astype(jnp.int32).reshape(1)
        for _ in range(max(1, spans - 1)):
            arriving = lax.ppermute(edge, "tm", backward)
            advantages, edge = advantage_stage(last, values, rewards, done_flags, boot, arriving)
        return values, advantages

    def padded():
        pool, where = exchange_slots(embedded, lists, capacity)
        return finish([attention(0, steps, {1: pool}, where + SPAN, own_projection())])

    if blocks != COLUMNS * ROWS or steps % 4:
        return padded()
    done, crowded = relay(embedded, lists, capacity, attention, own_projection)
    found = finish(done)
    return lax.cond(crowded > 0, padded, lambda: found)


def solution(mesh):
    placed = (
        P(("groups", "tm"), "agent", None),
        P(("groups", "agent"), "tm", None),
        P(("groups", "tm"), "agent"),
        P(("groups", "tm"), "agent"),
        P(("groups", "agent")),
        P(),
        P(),
        P(),
        P(),
        P(),
    )
    return jax.shard_map(
        body,
        mesh=mesh,
        in_specs=placed,
        out_specs=(P(("groups", "tm"), "agent"), P(("groups", "tm"), "agent")),
        check_vma=False,
    )
```

profile of v0, /device:TPU:0, one launch (start us, length us, event | category | flops | bytes accessed | tf_op | source)
XLA Modules:
  0.0 245.4 jit_solution(220661457461338180)
XLA Ops:
  1.5 3.0 %collective-permute-start.2 = (s32[32]{0:T(128)S(1)}, s32[32]{0:T(128)S(1)}, u32[]{:S(2)}, u32[]{:S(2)}) collective-permute-start(s32[32]{0:T(128)S(1)} %reshape_squeeze.7), channel_id=1, source_target_pairs={{0,2},{2,0},{4,6},{6,4},{8,10},{10,8},{12,14},{14,12},{1,3},{3,1},... | collective-permute-start | bytes 392 | tf_op jit(solution)/shard_map/ppermute | solution.py:636
  6.0 4.0 %collective-permute-start.3 = (s32[2,32]{1,0:T(2,128)S(1)}, s32[2,32]{1,0:T(2,128)S(1)}, u32[]{:S(2)}, u32[]{:S(2)}) collective-permute-start(s32[2,32]{1,0:T(2,128)S(1)} %pad_add_fusion.1), channel_id=1, source_target_pairs={{0,4},{2,6},{12,8},{14,10},{1,5},{3,7},{13,9},{15,11},{16,20},{18,... | collective-permute-start | bytes 776 | tf_op jit(solution)/shard_map/ppermute | solution.py:636
  12.8 2.3 collective-permute-start.4
  16.5 8.1 %plan.1 = (s32[77]{0:T(128)}, s32[32]{0:T(128)}, s32[1]{0:T(128)}) custom-call(s32[2]{0:T(128)} %pad_add_fusion.2.place_ref, s32[128]{0:T(128)} %copy-done.24), custom_call_target="tpu_custom_call" | custom-call | tf_op jit(solution)/shard_map/plan/pallas_call | solution.py:598
  25.2 1.9 pack.6.refs_4_
  27.2 1.9 collective-permute-start.6
  29.1 9.3 %collective-permute-done.6.refs_3_.refs_7_.refs_8_ = bf16[4,128,512]{2,1,0:T(8,128)(2,1)S(1)} collective-permute-done((bf16[4,128,512]{2,1,0:T(8,128)(2,1)S(1)}, bf16[4,128,512]{2,1,0:T(8,128)(2,1)S(1)}, u32[]{:S(2)}, u32[]{:S(2)}) %collective-permute-start.6) | collective-permute-done | bytes 524320 | tf_op jit(solution)/shard_map/ppermute | solution.py:636
  39.1 5.9 %pack.7 = (bf16[8,128,512]{2,1,0:T(8,128)(2,1)S(1)}, bf16[8,128,512]{2,1,0:T(8,128)(2,1)S(1)}, bf16[8,128,512]{2,1,0:T(8,128)(2,1)S(1)}) custom-call(s32[77]{0:T(128)S(1)} %copy-done.9, bf16[16,128,512]{2,1,0:T(8,128)(2,1)} %refs_0_.17, bf16[8,128,512]{2,1,0:T(8,128)(2,1)S(1)} %collective-permute-done.4.refs_1_, ...), custom_call_target="tpu_custom_call" | custom-call | bytes 65536 | tf_op jit(solution)/shard_map/pack/pallas_call | solution.py:226
  45.0 1.9 collective-permute-start.7
  49.2 4.3 %own_stage.3.refs_6_.projected_ref = bf16[16,128,1536]{2,1,0:T(8,128)(2,1)S(1)} custom-call(bf16[16,128,512]{2,1,0:T(8,128)(2,1)S(1)} %copy-done.12, bf16[512,1536]{1,0:T(8,128)(2,1)S(1)} %copy-done.15, bf16[8,128,512]{2,1,0:T(8,128)(2,1)S(1)} %get-tuple-element.72.refs_0_), custom_call_target="tpu_custom_call" | custom-call | tf_op jit(solution)/shard_map/own_stage/pallas_call | solution.py:79
  54.3 12.5 %collective-permute-done.7.refs_3_.refs_2_ = bf16[8,128,512]{2,1,0:T(8,128)(2,1)S(1)} collective-permute-done((bf16[8,128,512]{2,1,0:T(8,128)(2,1)S(1)}, bf16[8,128,512]{2,1,0:T(8,128)(2,1)S(1)}, u32[]{:S(2)}, u32[]{:S(2)}) %collective-permute-start.7) | collective-permute-done | bytes 1048608 | tf_op jit(solution)/shard_map/ppermute | solution.py:636
  66.7 2.9 %collective-permute-done.9.refs_5_.refs_8_.refs_9_ = bf16[8,128,512]{2,1,0:T(8,128)(2,1)S(1)} collective-permute-done((bf16[8,128,512]{2,1,0:T(8,128)(2,1)S(1)}, bf16[8,128,512]{2,1,0:T(8,128)(2,1)S(1)}, u32[]{:S(2)}, u32[]{:S(2)}) %collective-permute-start.9) | collective-permute-done | bytes 1048608 | tf_op jit(solution)/shard_map/ppermute | solution.py:636
  69.6 1.9 pack.8
  71.5 6.9 %collective-permute-start.10 = (bf16[8,128,512]{2,1,0:T(8,128)(2,1)S(1)}, bf16[8,128,512]{2,1,0:T(8,128)(2,1)S(1)}, u32[]{:S(2)}, u32[]{:S(2)}) collective-permute-start(bf16[8,128,512]{2,1,0:T(8,128)(2,1)S(1)} %get-tuple-element.73), channel_id=1, source_target_pairs={{0,4},{2,6},{4,0},{6,2},{8,12},{10,14},{12,8},{14,10},{1,5},{3,7},... | collective-permute-start | bytes 3145736 | tf_op jit(solution)/shard_map/ppermute | solution.py:636
  78.4 4.7 %collective-permute-start.13 = (bf16[8,128,512]{2,1,0:T(8,128)(2,1)S(1)}, bf16[8,128,512]{2,1,0:T(8,128)(2,1)S(1)}, u32[]{:S(2)}, u32[]{:S(2)}) collective-permute-start(bf16[8,128,512]{2,1,0:T(8,128)(2,1)S(1)} %get-tuple-element.75.refs_9_), channel_id=1, source_target_pairs={{0,2},{2,0},{4,6},{6,4},{8,10},{10,8},{12,14},{14,12},{1,3},{3,1},... | collective-permute-start | bytes 3145736 | tf_op jit(solution)/shard_map/ppermute | solution.py:636
  83.9 9.6 %collective-permute-done.10.refs_5_.refs_3_ = bf16[8,128,512]{2,1,0:T(8,128)(2,1)S(1)} collective-permute-done((bf16[8,128,512]{2,1,0:T(8,128)(2,1)S(1)}, bf16[8,128,512]{2,1,0:T(8,128)(2,1)S(1)}, u32[]{:S(2)}, u32[]{:S(2)}) %collective-permute-start.10) | collective-permute-done | bytes 1048608 | tf_op jit(solution)/shard_map/ppermute | solution.py:636
  93.6 4.3 %collective-permute-done.13.refs_8_.refs_9_.refs_10_ = bf16[8,128,512]{2,1,0:T(8,128)(2,1)S(1)} collective-permute-done((bf16[8,128,512]{2,1,0:T(8,128)(2,1)S(1)}, bf16[8,128,512]{2,1,0:T(8,128)(2,1)S(1)}, u32[]{:S(2)}, u32[]{:S(2)}) %collective-permute-start.13) | collective-permute-done | bytes 1048608 | tf_op jit(solution)/shard_map/ppermute | solution.py:636
  97.8 2.1 pack.9
  99.9 8.3 %collective-permute-start.14 = (bf16[8,128,512]{2,1,0:T(8,128)(2,1)S(1)}, bf16[8,128,512]{2,1,0:T(8,128)(2,1)S(1)}, u32[]{:S(2)}, u32[]{:S(2)}) collective-permute-start(bf16[8,128,512]{2,1,0:T(8,128)(2,1)S(1)} %get-tuple-element.76), channel_id=1, source_target_pairs={{0,4},{2,6},{4,0},{6,2},{8,12},{10,14},{12,8},{14,10},{1,5},{3,7},... | collective-permute-start | bytes 3145736 | tf_op jit(solution)/shard_map/ppermute | solution.py:636
  108.2 4.0 %collective-permute-start.16 = (bf16[7,128,512]{2,1,0:T(8,128)(2,1)S(1)}, bf16[7,128,512]{2,1,0:T(8,128)(2,1)S(1)}, u32[]{:S(2)}, u32[]{:S(2)}) collective-permute-start(bf16[7,128,512]{2,1,0:T(8,128)(2,1)S(1)} %get-tuple-element.77.refs_11_), channel_id=1, source_target_pairs={{0,2},{2,0},{4,6},{6,4},{8,10},{10,8},{12,14},{14,12},{1,3},{3,1},... | collective-permute-start | bytes 2752520 | tf_op jit(solution)/shard_map/ppermute | solution.py:636
  113.1 14.8 %collective-permute-done.16.refs_10_.refs_11_ = bf16[7,128,512]{2,1,0:T(8,128)(2,1)S(1)} collective-permute-done((bf16[7,128,512]{2,1,0:T(8,128)(2,1)S(1)}, bf16[7,128,512]{2,1,0:T(8,128)(2,1)S(1)}, u32[]{:S(2)}, u32[]{:S(2)}) %collective-permute-start.16) | collective-permute-done | bytes 917536 | tf_op jit(solution)/shard_map/ppermute | solution.py:636
  127.9 2.8 %pack.10 = (bf16[6,128,512]{2,1,0:T(8,128)(2,1)S(1)}, bf16[6,128,512]{2,1,0:T(8,128)(2,1)S(1)}) custom-call(s32[77]{0:T(128)S(1)} %copy-done.10, bf16[16,128,512]{2,1,0:T(8,128)(2,1)S(1)} %copy-done.12, bf16[8,128,512]{2,1,0:T(8,128)(2,1)S(1)} %collective-permute-done.4.refs_1_, bf16[8,128,512]{2,1,0:T(8,128)(2,1)S(1)} %collective-permute-done.5.refs_2_.refs_5_, ...), custom_call_target="tpu_custom_call" | custom-call | bytes 65536 | tf_op jit(solution)/shard_map/pack/pallas_call | solution.py:226
  131.6 4.7 %collective-permute-start.18 = (bf16[6,128,512]{2,1,0:T(8,128)(2,1)S(1)}, bf16[6,128,512]{2,1,0:T(8,128)(2,1)S(1)}, u32[]{:S(2)}, u32[]{:S(2)}) collective-permute-start(bf16[6,128,512]{2,1,0:T(8,128)(2,1)S(1)} %get-tuple-element.79.refs_11_), channel_id=1, source_target_pairs={{0,2},{2,0},{4,6},{6,4},{8,10},{10,8},{12,14},{14,12},{1,3},{3,1},... | collective-permute-start | bytes 2359304 | tf_op jit(solution)/shard_map/ppermute | solution.py:636
  136.3 16.7 %agent_stage.5 = (f32[8,128,512]{2,1,0:T(8,128)S(1)}, bf16[8,128,512]{2,1,0:T(8,128)(2,1)}) custom-call(s32[32]{0:T(128)S(1)} %copy-done.11, bf16[16,128,512]{2,1,0:T(8,128)(2,1)S(1)} %copy-done.12, bf16[16,128,1536]{2,1,0:T(8,128)(2,1)S(1)} %own_stage.3.refs_6_.projected_ref, bf16[16,128,512]{2,1,0:T(8,128)(2,1)S(1)} %copy-done.12, ...), custom_call_target="tpu_custom_call" | custom-call | flops 37580963840 | bytes 6291456 | tf_op jit(solution)/shard_map/agent_stage/pallas_call | solution.py:147
  153.0 2.3 collective-permute-start.20
  155.3 2.1 pack.11
  157.9 9.1 %agent_stage.6 = (f32[4,128,512]{2,1,0:T(8,128)S(1)}, bf16[4,128,512]{2,1,0:T(8,128)(2,1)}) custom-call(s32[32]{0:T(128)S(1)} %copy-done.11, bf16[16,128,512]{2,1,0:T(8,128)(2,1)S(1)} %copy-done.12, bf16[16,128,1536]{2,1,0:T(8,128)(2,1)S(1)} %own_stage.3.refs_6_.projected_ref, bf16[16,128,512]{2,1,0:T(8,128)(2,1)S(1)} %copy-done.12, ...), custom_call_target="tpu_custom_call" | custom-call | flops 18790481920 | bytes 3145728 | tf_op jit(solution)/shard_map/agent_stage/pallas_call | solution.py:147
  167.0 2.1 collective-permute-start.21
  169.6 9.2 %agent_stage.7 = (f32[4,128,512]{2,1,0:T(8,128)S(1)}, bf16[4,128,512]{2,1,0:T(8,128)(2,1)}) custom-call(s32[32]{0:T(128)S(1)} %copy-done.11, bf16[16,128,512]{2,1,0:T(8,128)(2,1)S(1)} %copy-done.12, bf16[16,128,1536]{2,1,0:T(8,128)(2,1)S(1)} %own_stage.3.refs_6_.projected_ref, bf16[16,128,512]{2,1,0:T(8,128)(2,1)S(1)} %copy-done.12, ...), custom_call_target="tpu_custom_call" | custom-call | flops 18790481920 | bytes 3145728 | tf_op jit(solution)/shard_map/agent_stage/pallas_call | solution.py:147
  181.2 1.7 collective-permute-done.22.refs_5_
  185.3 16.4 %time_stage.3 = (f32[16,128]{1,0:T(8,128)}, f32[2,128]{1,0:T(2,128)S(1)}) custom-call(s32[1]{0:T(128)} %bitcast.13.offset_ref, f32[8,128,512]{2,1,0:T(8,128)S(1)} %copy-done.1, f32[4,128,512]{2,1,0:T(8,128)S(1)} %copy-done.5, f32[4,128,512]{2,1,0:T(8,128)S(1)} %copy-done.7, bf16[8,128,512]{2,1,0:T(8,128)(2,1)} %collective-permute-done.20.refs_3_, ...), custom_call_target="tpu_custom_call" | custom-call | bytes 256 | tf_op jit(solution)/shard_map/time_stage/pallas_call | solution.py:341
  203.0 39.1 %all-gather = s32[256,128]{1,0:T(8,128)S(1)} all-gather(s32[8,128]{1,0:T(8,128)S(1)} %get-tuple-element.83), channel_id=2, replica_groups=mesh['groups'=2,'agent'=8,'tm'=2] {'groups','agent','tm'}, dimensions={0}, use_global_device_ids=true | all-gather | bytes 135168 | tf_op jit(solution)/shard_map/all_gather | solution.py:703
  (78 shorter events, 22.7 us)
Async XLA Ops:
  1.5 4.6 %collective-permute-start.2 = (s32[32]{0:T(128)S(1)}, s32[32]{0:T(128)S(1)}, u32[]{:S(2)}, u32[]{:S(2)}) collective-permute-start(s32[32]{0:T(128)S(1)} %reshape_squeeze.7), channel_id=1, source_target_pairs={{0,2},{2,0},{4,6},{6,4},{8,10},{10,8},{12,14},{14,12},{1,3},{3,1},... | collective-permute-start | bytes 392 | tf_op jit(solution)/shard_map/ppermute | solution.py:636
  6.0 5.3 %collective-permute-start.3 = (s32[2,32]{1,0:T(2,128)S(1)}, s32[2,32]{1,0:T(2,128)S(1)}, u32[]{:S(2)}, u32[]{:S(2)}) collective-permute-start(s32[2,32]{1,0:T(2,128)S(1)} %pad_add_fusion.1), channel_id=1, source_target_pairs={{0,4},{2,6},{12,8},{14,10},{1,5},{3,7},{13,9},{15,11},{16,20},{18,... | collective-permute-start | bytes 776 | tf_op jit(solution)/shard_map/ppermute | solution.py:636
  12.8 25.6 %collective-permute-start.4 = (bf16[8,128,512]{2,1,0:T(8,128)(2,1)S(1)}, bf16[8,128,512]{2,1,0:T(8,128)(2,1)S(1)}, u32[]{:S(2)}, u32[]{:S(2)}) collective-permute-start(bf16[8,128,512]{2,1,0:T(8,128)(2,1)S(1)} %constant_dynamic-slice_fusion), channel_id=1, source_target_pairs={{0,4},{2,6},{4,0},{6,2},{8,12},{10,14},{12,8},{14,10},{1,5},{3,7},... | collective-permute-start | bytes 3145736 | tf_op jit(solution)/shard_map/ppermute | solution.py:636
  15.2 23.3 %collective-permute-start.5 = (bf16[8,128,512]{2,1,0:T(8,128)(2,1)S(1)}, bf16[8,128,512]{2,1,0:T(8,128)(2,1)S(1)}, u32[]{:S(2)}, u32[]{:S(2)}) collective-permute-start(bf16[8,128,512]{2,1,0:T(8,128)(2,1)S(1)} %constant_dynamic-slice_fusion), channel_id=1, source_target_pairs={{4,8},{6,10},{8,4},{10,6},{5,9},{7,11},{9,5},{11,7},{20,24},{22,26... | collective-permute-start | bytes 3145736 | tf_op jit(solution)/shard_map/ppermute | solution.py:636
  25.2 24.0 %copy-start.12 = (bf16[16,128,512]{2,1,0:T(8,128)(2,1)S(1)}, bf16[16,128,512]{2,1,0:T(8,128)(2,1)}, u32[]{:S(2)}) copy-start(bf16[16,128,512]{2,1,0:T(8,128)(2,1)} %refs_0_.17) | copy-start | bytes 6291460
  27.2 11.3 %collective-permute-start.6 = (bf16[4,128,512]{2,1,0:T(8,128)(2,1)S(1)}, bf16[4,128,512]{2,1,0:T(8,128)(2,1)S(1)}, u32[]{:S(2)}, u32[]{:S(2)}) collective-permute-start(bf16[4,128,512]{2,1,0:T(8,128)(2,1)S(1)} %pack.6.refs_4_), channel_id=1, source_target_pairs={{0,2},{2,0},{4,6},{6,4},{8,10},{10,8},{12,14},{14,12},{1,3},{3,1},... | collective-permute-start | bytes 1572872 | tf_op jit(solution)/shard_map/ppermute | solution.py:636
  45.0 21.7 %collective-permute-start.7 = (bf16[8,128,512]{2,1,0:T(8,128)(2,1)S(1)}, bf16[8,128,512]{2,1,0:T(8,128)(2,1)S(1)}, u32[]{:S(2)}, u32[]{:S(2)}) collective-permute-start(bf16[8,128,512]{2,1,0:T(8,128)(2,1)S(1)} %get-tuple-element.71), channel_id=1, source_target_pairs={{0,4},{2,6},{4,0},{6,2},{8,12},{10,14},{12,8},{14,10},{1,5},{3,7},... | collective-permute-start | bytes 3145736 | tf_op jit(solution)/shard_map/ppermute | solution.py:636
  46.9 19.8 %collective-permute-start.8 = (bf16[8,128,512]{2,1,0:T(8,128)(2,1)S(1)}, bf16[8,128,512]{2,1,0:T(8,128)(2,1)S(1)}, u32[]{:S(2)}, u32[]{:S(2)}) collective-permute-start(bf16[8,128,512]{2,1,0:T(8,128)(2,1)S(1)} %collective-permute-done.4.refs_1_), channel_id=1, source_target_pairs={{4,8},{6,10},{8,4},{10,6},{5,9},{7,11},{9,5},{11,7},{20,24},{22,26... | collective-permute-start | bytes 3145736 | tf_op jit(solution)/shard_map/ppermute | solution.py:636
  47.6 22.0 %copy-start.10 = (s32[77]{0:T(128)S(1)}, s32[77]{0:T(128)}, u32[]{:S(2)}) copy-start(s32[77]{0:T(128)} %get-tuple-element.70.table_ref) | copy-start | bytes 928
  47.6 22.0 %collective-permute-start.9 = (bf16[8,128,512]{2,1,0:T(8,128)(2,1)S(1)}, bf16[8,128,512]{2,1,0:T(8,128)(2,1)S(1)}, u32[]{:S(2)}, u32[]{:S(2)}) collective-permute-start(bf16[8,128,512]{2,1,0:T(8,128)(2,1)S(1)} %get-tuple-element.72.refs_0_), channel_id=1, source_target_pairs={{0,2},{2,0},{4,6},{6,4},{8,10},{10,8},{12,14},{14,12},{1,3},{3,1},... | collective-permute-start | bytes 3145736 | tf_op jit(solution)/shard_map/ppermute | solution.py:636
  53.5 30.4 %collective-permute-start.11 = (bf16[8,128,512]{2,1,0:T(8,128)(2,1)S(1)}, bf16[8,128,512]{2,1,0:T(8,128)(2,1)S(1)}, u32[]{:S(2)}, u32[]{:S(2)}) collective-permute-start(bf16[8,128,512]{2,1,0:T(8,128)(2,1)S(1)} %get-tuple-element.74), channel_id=1, source_target_pairs={{4,8},{6,10},{8,4},{10,6},{5,9},{7,11},{9,5},{11,7},{20,24},{22,26... | collective-permute-start | bytes 3145736 | tf_op jit(solution)/shard_map/ppermute | solution.py:636
  71.5 22.0 %collective-permute-start.10 = (bf16[8,128,512]{2,1,0:T(8,128)(2,1)S(1)}, bf16[8,128,512]{2,1,0:T(8,128)(2,1)S(1)}, u32[]{:S(2)}, u32[]{:S(2)}) collective-permute-start(bf16[8,128,512]{2,1,0:T(8,128)(2,1)S(1)} %get-tuple-element.73), channel_id=1, source_target_pairs={{0,4},{2,6},{4,0},{6,2},{8,12},{10,14},{12,8},{14,10},{1,5},{3,7},... | collective-permute-start | bytes 3145736 | tf_op jit(solution)/shard_map/ppermute | solution.py:636
  78.4 19.4 %collective-permute-start.13 = (bf16[8,128,512]{2,1,0:T(8,128)(2,1)S(1)}, bf16[8,128,512]{2,1,0:T(8,128)(2,1)S(1)}, u32[]{:S(2)}, u32[]{:S(2)}) collective-permute-start(bf16[8,128,512]{2,1,0:T(8,128)(2,1)S(1)} %get-tuple-element.75.refs_9_), channel_id=1, source_target_pairs={{0,2},{2,0},{4,6},{6,4},{8,10},{10,8},{12,14},{14,12},{1,3},{3,1},... | collective-permute-start | bytes 3145736 | tf_op jit(solution)/shard_map/ppermute | solution.py:636
  83.2 0.7 collective-permute-start.12
  99.9 28.0 %collective-permute-start.14 = (bf16[8,128,512]{2,1,0:T(8,128)(2,1)S(1)}, bf16[8,128,512]{2,1,0:T(8,128)(2,1)S(1)}, u32[]{:S(2)}, u32[]{:S(2)}) collective-permute-start(bf16[8,128,512]{2,1,0:T(8,128)(2,1)S(1)} %get-tuple-element.76), channel_id=1, source_target_pairs={{0,4},{2,6},{4,0},{6,2},{8,12},{10,14},{12,8},{14,10},{1,5},{3,7},... | collective-permute-start | bytes 3145736 | tf_op jit(solution)/shard_map/ppermute | solution.py:636
  108.2 19.6 %collective-permute-start.16 = (bf16[7,128,512]{2,1,0:T(8,128)(2,1)S(1)}, bf16[7,128,512]{2,1,0:T(8,128)(2,1)S(1)}, u32[]{:S(2)}, u32[]{:S(2)}) collective-permute-start(bf16[7,128,512]{2,1,0:T(8,128)(2,1)S(1)} %get-tuple-element.77.refs_11_), channel_id=1, source_target_pairs={{0,2},{2,0},{4,6},{6,4},{8,10},{10,8},{12,14},{14,12},{1,3},{3,1},... | collective-permute-start | bytes 2752520 | tf_op jit(solution)/shard_map/ppermute | solution.py:636
  112.3 24.0 %copy-start.11 = (s32[32]{0:T(128)S(1)}, s32[32]{0:T(128)}, u32[]{:S(2)}) copy-start(s32[32]{0:T(128)} %get-tuple-element.80.table_ref) | copy-start | bytes 388
  112.3 24.0 %copy-start.25 = (bf16[512,512]{1,0:T(8,128)(2,1)S(1)}, bf16[512,512]{1,0:T(8,128)(2,1)}, u32[]{:S(2)}) copy-start(bf16[512,512]{1,0:T(8,128)(2,1)} %refs_16_.1) | copy-start | bytes 1572868
  112.3 0.8 collective-permute-start.15
  130.7 24.6 %collective-permute-start.17 = (bf16[6,128,512]{2,1,0:T(8,128)(2,1)S(1)}, bf16[6,128,512]{2,1,0:T(8,128)(2,1)S(1)}, u32[]{:S(2)}, u32[]{:S(2)}) collective-permute-start(bf16[6,128,512]{2,1,0:T(8,128)(2,1)S(1)} %get-tuple-element.78), channel_id=1, source_target_pairs={{0,4},{2,6},{4,0},{6,2},{8,12},{10,14},{12,8},{14,10},{1,5},{3,7},... | collective-permute-start | bytes 2359304 | tf_op jit(solution)/shard_map/ppermute | solution.py:636
  131.6 23.8 %collective-permute-start.18 = (bf16[6,128,512]{2,1,0:T(8,128)(2,1)S(1)}, bf16[6,128,512]{2,1,0:T(8,128)(2,1)S(1)}, u32[]{:S(2)}, u32[]{:S(2)}) collective-permute-start(bf16[6,128,512]{2,1,0:T(8,128)(2,1)S(1)} %get-tuple-element.79.refs_11_), channel_id=1, source_target_pairs={{0,2},{2,0},{4,6},{6,4},{8,10},{10,8},{12,14},{14,12},{1,3},{3,1},... | collective-permute-start | bytes 2359304 | tf_op jit(solution)/shard_map/ppermute | solution.py:636
  153.0 28.1 %collective-permute-start.20 = (bf16[8,128,512]{2,1,0:T(8,128)(2,1)}, bf16[8,128,512]{2,1,0:T(8,128)(2,1)}, u32[]{:S(2)}, u32[]{:S(2)}) collective-permute-start(bf16[8,128,512]{2,1,0:T(8,128)(2,1)} %get-tuple-element.87), channel_id=1, source_target_pairs={{0,1},{2,3},{4,5},{6,7},{8,9},{10,11},{12,13},{14,15},{16,17},{18,... | collective-permute-start | bytes 3145736 | tf_op jit(solution)/shard_map/ppermute | solution.py:755
  157.5 12.1 %collective-permute-start.19 = (bf16[6,128,512]{2,1,0:T(8,128)(2,1)S(1)}, bf16[6,128,512]{2,1,0:T(8,128)(2,1)S(1)}, u32[]{:S(2)}, u32[]{:S(2)}) collective-permute-start(bf16[6,128,512]{2,1,0:T(8,128)(2,1)S(1)} %get-tuple-element.84.refs_13_), channel_id=1, source_target_pairs={{0,2},{2,0},{4,6},{6,4},{8,10},{10,8},{12,14},{14,12},{1,3},{3,1},... | collective-permute-start | bytes 2359304 | tf_op jit(solution)/shard_map/ppermute | solution.py:636
  167.0 14.1 %collective-permute-start.21 = (bf16[4,128,512]{2,1,0:T(8,128)(2,1)}, bf16[4,128,512]{2,1,0:T(8,128)(2,1)}, u32[]{:S(2)}, u32[]{:S(2)}) collective-permute-start(bf16[4,128,512]{2,1,0:T(8,128)(2,1)} %get-tuple-element.88), channel_id=1, source_target_pairs={{0,1},{2,3},{4,5},{6,7},{8,9},{10,11},{12,13},{14,15},{16,17},{18,... | collective-permute-start | bytes 1572872 | tf_op jit(solution)/shard_map/ppermute | solution.py:755
  169.6 13.3 %copy-start.1 = (f32[8,128,512]{2,1,0:T(8,128)S(1)}, f32[8,128,512]{2,1,0:T(8,128)}, u32[]{:S(2)}) copy-start(f32[8,128,512]{2,1,0:T(8,128)} %copy-done) | copy-start | bytes 6291460
  169.6 13.3 %copy-start.17 = (s32[16,128]{1,0:T(8,128)S(1)}, s32[16,128]{1,0:T(8,128)}, u32[]{:S(2)}) copy-start(s32[16,128]{1,0:T(8,128)} %done_ref.1) | copy-start | bytes 24580
  169.6 13.3 %copy-start.18 = (f32[16,128]{1,0:T(8,128)S(1)}, f32[16,128]{1,0:T(8,128)}, u32[]{:S(2)}) copy-start(f32[16,128]{1,0:T(8,128)} %rewards_ref.1) | copy-start | bytes 24580
  169.6 13.3 %copy-start.19 = (f32[512]{0:T(512)S(1)}, f32[512]{0:T(512)}, u32[]{:S(2)}) copy-start(f32[512]{0:T(512)} %param.21) | copy-start | bytes 6148
  169.6 13.3 %copy-start.20 = (f32[128]{0:T(128)S(1)}, f32[128]{0:T(128)}, u32[]{:S(2)}) copy-start(f32[128]{0:T(128)} %param.16) | copy-start | bytes 1540
  179.8 3.0 %collective-permute-start.22 = (bf16[4,128,512]{2,1,0:T(8,128)(2,1)}, bf16[4,128,512]{2,1,0:T(8,128)(2,1)S(1)}, u32[]{:S(2)}, u32[]{:S(2)}) collective-permute-start(bf16[4,128,512]{2,1,0:T(8,128)(2,1)} %get-tuple-element.89), channel_id=1, source_target_pairs={{0,1},{2,3},{4,5},{6,7},{8,9},{10,11},{12,13},{14,15},{16,17},{18,... | collective-permute-start | bytes 1572872 | tf_op jit(solution)/shard_map/ppermute | solution.py:755
  185.3 60.1 %copy-start.21 = (s32[1,16,2]{1,2,0:T(2,128)S(1)}, s32[1,16,2]{1,2,0:T(2,128)}, u32[]{:S(2)}) copy-start(s32[1,16,2]{1,2,0:T(2,128)} %param.13) | copy-start | bytes 388
  201.7 41.7 %collective-permute-start.23 = (f32[2,128]{1,0:T(2,128)S(1)}, f32[2,128]{1,0:T(2,128)S(1)}, u32[]{:S(2)}, u32[]{:S(2)}) collective-permute-start(f32[2,128]{1,0:T(2,128)S(1)} %get-tuple-element.91), channel_id=1, source_target_pairs={{1,0},{3,2},{5,4},{7,6},{9,8},{11,10},{13,12},{15,14},{17,16},{19,... | collective-permute-start | bytes 3080 | tf_op jit(solution)/shard_map/ppermute | solution.py:772
  (10 other events, 36.8 us)
where the time goes:
time: 247 us; the launch traced here: 245 us
  Pallas kernels  81.9 us (33%)
  waiting for transfers between devices  58.3 us (24%)
  starting transfers between devices  55.3 us (22%)
  blocking collectives  39.1 us (16%)
  local copies, waits for them, and re-layouts  7.68 us (3%)
    ppermute x18, waiting for transfers between devices, relay(): send = lambda value, pairs: lax.ppermute(value, 'agent', pairs)  56.6 us
    ppermute x18, starting transfers between devices, relay(): send = lambda value, pairs: lax.ppermute(value, 'agent', pairs)  48.4 us
    all_gather x1, blocking collectives, relay(): crowded = jnp.max(lax.all_gather(packed[-1], ('groups', 'agent', 'tm')))  39.1 us
    pallas_call x3, Pallas kernels, agent_stage(): pl.pallas_call(functools.partial(agent_kernel, list_length, first_step, t...  35 us
    pallas_call x6, Pallas kernels, pack(): pl.pallas_call(functools.partial(pack_kernel, tuple(arrays), tuple(parts)...  16.8 us
    pallas_call x1, Pallas kernels, time_stage(): pl.pallas_call(functools.partial(time_kernel, len(residuals), steps, tile...  16.4 us
    pallas_call x1, Pallas kernels, plan(): pl.pallas_call(functools.partial(plan_kernel, steps, list_length, chunks,...  8.07 us
    unnamed x41, local copies, waits for them, and re-layouts  6.11 us
  transfers between devices with their start and end apart: 22, of which 10 were waited for; matrix products, arithmetic and copies ran while one was open for 1% of the time, Pallas kernels for 22%

commit v1 on v0

--- a/solution.py
+++ b/solution.py
@@ -86,7 +86,7 @@
         + [pl.BlockSpec(memory_space=pltpu.HBM)] * len(after),
         out_specs=pl.BlockSpec((together, agents, proj.shape[1]), lambda i: (i, 0, 0)),
         out_shape=jax.ShapeDtypeStruct((steps, agents, proj.shape[1]), bf16),
-        compiler_params=pltpu.CompilerParams(vmem_limit_bytes=20 * MIB),
+        compiler_params=pltpu.CompilerParams(vmem_limit_bytes=18 * MIB),
         name="own_stage",
     )(embedded, proj, *after)
 
@@ -167,7 +167,7 @@
             jax.ShapeDtypeStruct((steps, agents, width), f32),
             jax.ShapeDtypeStruct((steps, agents, width), bf16),
         ],
-        compiler_params=pltpu.CompilerParams(vmem_limit_bytes=24 * MIB),
+        compiler_params=pltpu.CompilerParams(vmem_limit_bytes=18 * MIB),
         cost_estimate=pl.CostEstimate(
             flops=5 * flops, bytes_accessed=steps * agents * width * 12, transcendentals=0
         ),
@@ -175,12 +175,9 @@
     )(table, embedded, projected, *arrays.values(), *after, proj, merge)
 
 
-def pack_kernel(codes, parts, idle, flagged, table_ref, *refs):
+def pack_kernel(codes, parts, idle, table_ref, *refs):
     arrays = dict(zip(codes, refs))
     outs, (held_ref, in_sems, out_sems) = refs[len(codes) + idle : -3], refs[-3:]
-    if flagged:
-        outs[-1][...] = jnp.full(outs[-1].shape, outs[0][0], jnp.int32)
-        outs = outs[1:-1]
     slots = []
     for out, (offset, count, first) in zip(outs, parts):
         slots += [(offset, first, n, out.at[n]) for n in range(count)]
@@ -212,20 +209,16 @@
         guarded(offset, n, finish)
 
 
-def pack(table, arrays, parts, after=(), flag=None):
+def pack(table, arrays, parts, after=()):
     piece = next(iter(arrays.values())).shape[1:]
     slots = sum(count for _, count, _ in parts)
     smem = pl.BlockSpec(memory_space=pltpu.SMEM)
     hbm = pl.BlockSpec(memory_space=pltpu.HBM)
-    flags = () if flag is None else (flag,)
     out_specs = [hbm] * len(parts)
     out_shape = [jax.ShapeDtypeStruct((count,) + piece, bf16) for _, count, _ in parts]
-    if flags:
-        out_specs.append(pl.BlockSpec(memory_space=pltpu.VMEM))
-        out_shape.append(jax.ShapeDtypeStruct((8, 128), jnp.int32))
     return pl.pallas_call(
-        functools.partial(pack_kernel, tuple(arrays), tuple(parts), len(after), len(flags)),
-        in_specs=[smem] + [hbm] * (len(arrays) + len(after)) + [smem] * len(flags),
+        functools.partial(pack_kernel, tuple(arrays), tuple(parts), len(after)),
+        in_specs=[smem] + [hbm] * (len(arrays) + len(after)),
         out_specs=out_specs,
         out_shape=out_shape,
         scratch_shapes=[
@@ -240,7 +233,7 @@
             vmem_limit_bytes=slots * piece[0] * piece[1] * 2 + 2 * MIB
         ),
         name="pack",
-    )(table, *arrays.values(), *after, *flags)
+    )(table, *arrays.values(), *after)
 
 
 def suffix(values, rewards, done, next_value, next_advantage):
@@ -356,7 +349,7 @@
             jax.ShapeDtypeStruct((steps, agents), f32),
             jax.ShapeDtypeStruct((2, agents), f32),
         ],
-        compiler_params=pltpu.CompilerParams(vmem_limit_bytes=28 * MIB),
+        compiler_params=pltpu.CompilerParams(vmem_limit_bytes=20 * MIB),
         cost_estimate=pl.CostEstimate(flops=0, bytes_accessed=rows, transcendentals=0),
         name="time_stage",
     )(offset, *residuals, *rims, *fixed)
@@ -646,14 +639,14 @@
     def across_part(n):
         return (y_base[n], across[n], None)
 
-    def stage(n, reads, settled, after=(), flag=None):
+    def stage(n, reads, settled, after=()):
         parts = [across_part(n)]
         if n < len(outward):
             parts.append((e_base[n], outward[n], None))
         if n == 1:
             parts.append((None, outward[1], starts[1]))
         after = tuple(arrays[rows[b]] for b in settled) + tuple(after)
-        packed = pack(out_table, pick([own] + reads), parts, after, flag)
+        packed = pack(out_table, pick([own] + reads), parts, after)
         if n < len(outward):
             arrays[edge[n]] = send(packed[1], edges)
         arrays[rows[n]] = send(packed[0], over)
@@ -676,9 +669,10 @@
     )
     (token,) = pack(out_table, pick([own]), [across_part(0)])
     arrays[rows[0]] = send(token, over)
+    crowded = jnp.max(shared(flag, ("groups", "agent", "tm")))
     arrays[far[0]] = send(arrays[edge[0]], swap)
     reads = edge[:1] + swapped[:1]
-    packed = stage(1, reads, (0,), (token,))
+    packed = stage(1, reads, (0,), (token, crowded.reshape(1)))
     arrays[swapped[1]] = send(packed[2], swap)
     for k in (1, 2):
         at = starts[k] - starts[1]
@@ -698,9 +692,8 @@
 
     done = [attend_chunk(0, packed[:1])]
     reads = reads + edge[4:5]
-    packed = stage(5, reads, (4,), (done[0][0],), flag)
+    packed = stage(5, reads, (4,), (done[0][0],))
     done.append(attend_chunk(1, packed[:1]))
-    crowded = jnp.max(lax.all_gather(packed[-1], ("groups", "agent", "tm")))
     done.append(attend_chunk(2, (done[1][0],)))
     return done, crowded
 

time: 247 us -> 222 us (0.90)
  blocking collectives: 39.1 us -> 12 us
  starting transfers between devices: 55.3 us -> 42.5 us
  waiting for transfers between devices: 58.3 us -> 70.1 us
  local copies, waits for them, and re-layouts: 7.68 us -> 10.4 us
    all_gather x1 -> x0, blocking collectives: 39.1 us -> none  [relay(): crowded = jnp.max(lax.all_gather(packed[-1], ('groups', 'agent', 'tm')))]
    ppermute x18, starting transfers between devices: 48.4 us -> 35.5 us  [relay(): send = lambda value, pairs: lax.ppermute(value, 'agent', pairs)]
    all_to_all x0 -> x1, blocking collectives: none -> 12 us  [shared(): return lax.all_to_all(rows, axes, split_axis=0, concat_axis=0, tiled=True)]
    ppermute x18, waiting for transfers between devices: 56.6 us -> 67.4 us  [relay(): send = lambda value, pairs: lax.ppermute(value, 'agent', pairs)]
    unnamed x41 -> x45, local copies, waits for them, and re-layouts: 6.11 us -> 7.18 us
  transfers between devices with their start and end apart: 22 -> 22, of which waited for: 10 -> 11; matrix products, arithmetic and copies ran while one was open for 1% -> 1% of each run, Pallas kernels for 22% -> 24%
where the time goes in v1:
time: 222 us; the launch traced here: 221 us
  Pallas kernels  82.6 us (37%)
  waiting for transfers between devices  70.1 us (32%)
  starting transfers between devices  42.5 us (19%)
  blocking collectives  12 us (5%)
  local copies, waits for them, and re-layouts  10.4 us (5%)
    ppermute x18, waiting for transfers between devices, relay(): send = lambda value, pairs: lax.ppermute(value, 'agent', pairs)  67.4 us
    ppermute x18, starting transfers between devices, relay(): send = lambda value, pairs: lax.ppermute(value, 'agent', pairs)  35.5 us
    pallas_call x3, Pallas kernels, agent_stage(): pl.pallas_call(functools.partial(agent_kernel, list_length, first_step, t...  34.7 us
    pallas_call x6, Pallas kernels, pack(): pl.pallas_call(functools.partial(pack_kernel, tuple(arrays), tuple(parts)...  17.8 us
    pallas_call x1, Pallas kernels, time_stage(): pl.pallas_call(functools.partial(time_kernel, len(residuals), steps, tile...  16.4 us
    all_to_all x1, blocking collectives, shared(): return lax.all_to_all(rows, axes, split_axis=0, concat_axis=0, tiled=True)  12 us
    pallas_call x1, Pallas kernels, plan(): pl.pallas_call(functools.partial(plan_kernel, steps, list_length, chunks,...  8.07 us
    unnamed x45, local copies, waits for them, and re-layouts  7.18 us
  transfers between devices with their start and end apart: 22, of which 11 were waited for; matrix products, arithmetic and copies ran while one was open for 1% of the time, Pallas kernels for 24%

profile of v1, /device:TPU:0, one launch (start us, length us, event | category | flops | bytes accessed | tf_op | source)
XLA Modules:
  0.0 220.7 jit_solution(6546763253302487991)
XLA Ops:
  1.5 3.0 %collective-permute-start.2 = (s32[32]{0:T(128)S(1)}, s32[32]{0:T(128)S(1)}, u32[]{:S(2)}, u32[]{:S(2)}) collective-permute-start(s32[32]{0:T(128)S(1)} %reshape_squeeze.7), channel_id=1, source_target_pairs={{0,2},{2,0},{4,6},{6,4},{8,10},{10,8},{12,14},{14,12},{1,3},{3,1},... | collective-permute-start | bytes 392 | tf_op jit(solution)/shard_map/ppermute | solution.py:629
  4.5 1.5 collective-permute-done.2
  6.0 4.0 %collective-permute-start.3 = (s32[2,32]{1,0:T(2,128)S(1)}, s32[2,32]{1,0:T(2,128)S(1)}, u32[]{:S(2)}, u32[]{:S(2)}) collective-permute-start(s32[2,32]{1,0:T(2,128)S(1)} %pad_add_fusion.1), channel_id=1, source_target_pairs={{0,4},{2,6},{12,8},{14,10},{1,5},{3,7},{13,9},{15,11},{16,20},{18,... | collective-permute-start | bytes 776 | tf_op jit(solution)/shard_map/ppermute | solution.py:629
  11.5 2.3 %constant_dynamic-slice_fusion = bf16[8,128,512]{2,1,0:T(8,128)(2,1)} fusion(bf16[16,128,512]{2,1,0:T(8,128)(2,1)} %refs_0_.17, s32[]{:T(128)S(6)} %select_n.68), kind=kLoop, calls=%fused_computation.24 | loop fusion | bytes 2097156 | tf_op jit(solution)/shard_map/dynamic_slice | solution.py:664
  13.8 2.3 %collective-permute-start.4 = (bf16[8,128,512]{2,1,0:T(8,128)(2,1)}, bf16[8,128,512]{2,1,0:T(8,128)(2,1)S(1)}, u32[]{:S(2)}, u32[]{:S(2)}) collective-permute-start(bf16[8,128,512]{2,1,0:T(8,128)(2,1)} %constant_dynamic-slice_fusion), channel_id=1, source_target_pairs={{0,4},{2,6},{4,0},{6,2},{8,12},{10,14},{12,8},{14,10},{1,5},{3,7},... | collective-permute-start | bytes 3145736 | tf_op jit(solution)/shard_map/ppermute | solution.py:629
  17.4 8.1 %plan.1 = (s32[77]{0:T(128)}, s32[32]{0:T(128)}, s32[1]{0:T(128)}) custom-call(s32[2]{0:T(128)} %pad_add_fusion.2.place_ref, s32[128]{0:T(128)} %copy-done.26), custom_call_target="tpu_custom_call" | custom-call | tf_op jit(solution)/shard_map/plan/pallas_call | solution.py:591
  26.2 2.2 pack.6.refs_4_
  30.3 12.0 %all_to_all.18 = s32[32,1,1]{2,1,0:T(1,128)S(1)} all-to-all(s32[32,1,1]{2,1,0:T(1,128)S(1)} %broadcast_in_dim.5), channel_id=1, replica_groups=mesh['groups'=2,'agent'=8,'tm'=2] {'groups','agent','tm'}, dimensions={0} | all-to-all | bytes 256 | tf_op jit(solution)/shard_map/all_to_all | solution.py:612
  43.8 6.3 %pack.7 = (bf16[8,128,512]{2,1,0:T(8,128)(2,1)S(1)}, bf16[8,128,512]{2,1,0:T(8,128)(2,1)S(1)}, bf16[8,128,512]{2,1,0:T(8,128)(2,1)S(1)}) custom-call(s32[77]{0:T(128)S(1)} %copy-done.11, bf16[16,128,512]{2,1,0:T(8,128)(2,1)} %refs_0_.17, bf16[8,128,512]{2,1,0:T(8,128)(2,1)S(1)} %collective-permute-done.4.refs_1_, ...), custom_call_target="tpu_custom_call" | custom-call | bytes 65536 | tf_op jit(solution)/shard_map/pack/pallas_call | solution.py:219
  50.1 2.6 %collective-permute-start.7 = (bf16[8,128,512]{2,1,0:T(8,128)(2,1)S(1)}, bf16[8,128,512]{2,1,0:T(8,128)(2,1)S(1)}, u32[]{:S(2)}, u32[]{:S(2)}) collective-permute-start(bf16[8,128,512]{2,1,0:T(8,128)(2,1)S(1)} %get-tuple-element.72), channel_id=1, source_target_pairs={{0,4},{2,6},{4,0},{6,2},{8,12},{10,14},{12,8},{14,10},{1,5},{3,7},... | collective-permute-start | bytes 3145736 | tf_op jit(solution)/shard_map/ppermute | solution.py:629
  53.9 4.3 %own_stage.3.refs_6_.projected_ref = bf16[16,128,1536]{2,1,0:T(8,128)(2,1)S(1)} custom-call(bf16[16,128,512]{2,1,0:T(8,128)(2,1)S(1)} %copy-done.14, bf16[512,1536]{1,0:T(8,128)(2,1)S(1)} %copy-done.17, bf16[8,128,512]{2,1,0:T(8,128)(2,1)S(1)} %get-tuple-element.71.refs_0_), custom_call_target="tpu_custom_call" | custom-call | tf_op jit(solution)/shard_map/own_stage/pallas_call | solution.py:79
  58.9 16.9 %collective-permute-done.7.refs_3_.refs_2_ = bf16[8,128,512]{2,1,0:T(8,128)(2,1)S(1)} collective-permute-done((bf16[8,128,512]{2,1,0:T(8,128)(2,1)S(1)}, bf16[8,128,512]{2,1,0:T(8,128)(2,1)S(1)}, u32[]{:S(2)}, u32[]{:S(2)}) %collective-permute-start.7) | collective-permute-done | bytes 1048608 | tf_op jit(solution)/shard_map/ppermute | solution.py:629
  75.8 1.5 collective-permute-done.9.refs_5_.refs_8_.refs_9_
  77.3 3.3 %pack.8 = (bf16[8,128,512]{2,1,0:T(8,128)(2,1)S(1)}, bf16[8,128,512]{2,1,0:T(8,128)(2,1)S(1)}) custom-call(s32[77]{0:T(128)S(1)} %copy-done.12, bf16[16,128,512]{2,1,0:T(8,128)(2,1)S(1)} %copy-done.14, bf16[8,128,512]{2,1,0:T(8,128)(2,1)S(1)} %collective-permute-done.4.refs_1_, bf16[8,128,512]{2,1,0:T(8,128)(2,1)S(1)} %collective-permute-done.5.refs_2_.refs_5_, ...), custom_call_target="tpu_custom_call" | custom-call | bytes 65536 | tf_op jit(solution)/shard_map/pack/pallas_call | solution.py:219
  80.6 5.0 %collective-permute-start.10 = (bf16[8,128,512]{2,1,0:T(8,128)(2,1)S(1)}, bf16[8,128,512]{2,1,0:T(8,128)(2,1)S(1)}, u32[]{:S(2)}, u32[]{:S(2)}) collective-permute-start(bf16[8,128,512]{2,1,0:T(8,128)(2,1)S(1)} %get-tuple-element.73), channel_id=1, source_target_pairs={{0,4},{2,6},{4,0},{6,2},{8,12},{10,14},{12,8},{14,10},{1,5},{3,7},... | collective-permute-start | bytes 3145736 | tf_op jit(solution)/shard_map/ppermute | solution.py:629
  86.4 19.6 %collective-permute-done.10.refs_5_.refs_3_ = bf16[8,128,512]{2,1,0:T(8,128)(2,1)S(1)} collective-permute-done((bf16[8,128,512]{2,1,0:T(8,128)(2,1)S(1)}, bf16[8,128,512]{2,1,0:T(8,128)(2,1)S(1)}, u32[]{:S(2)}, u32[]{:S(2)}) %collective-permute-start.10) | collective-permute-done | bytes 1048608 | tf_op jit(solution)/shard_map/ppermute | solution.py:629
  106.0 1.5 collective-permute-done.13.refs_8_.refs_9_.refs_10_
  107.5 2.1 pack.9
  109.6 8.6 %collective-permute-start.14 = (bf16[8,128,512]{2,1,0:T(8,128)(2,1)S(1)}, bf16[8,128,512]{2,1,0:T(8,128)(2,1)S(1)}, u32[]{:S(2)}, u32[]{:S(2)}) collective-permute-start(bf16[8,128,512]{2,1,0:T(8,128)(2,1)S(1)} %get-tuple-element.76), channel_id=1, source_target_pairs={{0,4},{2,6},{4,0},{6,2},{8,12},{10,14},{12,8},{14,10},{1,5},{3,7},... | collective-permute-start | bytes 3145736 | tf_op jit(solution)/shard_map/ppermute | solution.py:629
  119.7 19.2 %collective-permute-done.15.refs_10_.refs_11_ = bf16[7,128,512]{2,1,0:T(8,128)(2,1)S(1)} collective-permute-done((bf16[7,128,512]{2,1,0:T(8,128)(2,1)S(1)}, bf16[7,128,512]{2,1,0:T(8,128)(2,1)S(1)}, u32[]{:S(2)}, u32[]{:S(2)}) %collective-permute-start.15) | collective-permute-done | bytes 917536 | tf_op jit(solution)/shard_map/ppermute | solution.py:629
  140.2 2.5 %pack.10 = (bf16[6,128,512]{2,1,0:T(8,128)(2,1)S(1)}, bf16[6,128,512]{2,1,0:T(8,128)(2,1)S(1)}) custom-call(s32[77]{0:T(128)S(1)} %copy-done.12, bf16[16,128,512]{2,1,0:T(8,128)(2,1)S(1)} %copy-done.14, bf16[8,128,512]{2,1,0:T(8,128)(2,1)S(1)} %collective-permute-done.4.refs_1_, bf16[8,128,512]{2,1,0:T(8,128)(2,1)S(1)} %collective-permute-done.5.refs_2_.refs_5_, ...), custom_call_target="tpu_custom_call" | custom-call | bytes 65536 | tf_op jit(solution)/shard_map/pack/pallas_call | solution.py:219
  142.7 1.8 collective-permute-start.17
  145.7 16.6 %agent_stage.5 = (f32[8,128,512]{2,1,0:T(8,128)S(1)}, bf16[8,128,512]{2,1,0:T(8,128)(2,1)}) custom-call(s32[32]{0:T(128)S(1)} %copy-done.13, bf16[16,128,512]{2,1,0:T(8,128)(2,1)S(1)} %copy-done.14, bf16[16,128,1536]{2,1,0:T(8,128)(2,1)S(1)} %own_stage.3.refs_6_.projected_ref, bf16[16,128,512]{2,1,0:T(8,128)(2,1)S(1)} %copy-done.14, ...), custom_call_target="tpu_custom_call" | custom-call | flops 37580963840 | bytes 6291456 | tf_op jit(solution)/shard_map/agent_stage/pallas_call | solution.py:147
  162.3 2.3 %collective-permute-start.20 = (bf16[8,128,512]{2,1,0:T(8,128)(2,1)}, bf16[8,128,512]{2,1,0:T(8,128)(2,1)}, u32[]{:S(2)}, u32[]{:S(2)}) collective-permute-start(bf16[8,128,512]{2,1,0:T(8,128)(2,1)} %get-tuple-element.83), channel_id=1, source_target_pairs={{0,1},{2,3},{4,5},{6,7},{8,9},{10,11},{12,13},{14,15},{16,17},{18,... | collective-permute-start | bytes 3145736 | tf_op jit(solution)/shard_map/ppermute | solution.py:748
  164.6 1.5 pack.11.refs_13_
  167.0 9.0 %agent_stage.6 = (f32[4,128,512]{2,1,0:T(8,128)S(1)}, bf16[4,128,512]{2,1,0:T(8,128)(2,1)}) custom-call(s32[32]{0:T(128)S(1)} %copy-done.13, bf16[16,128,512]{2,1,0:T(8,128)(2,1)S(1)} %copy-done.14, bf16[16,128,1536]{2,1,0:T(8,128)(2,1)S(1)} %own_stage.3.refs_6_.projected_ref, bf16[16,128,512]{2,1,0:T(8,128)(2,1)S(1)} %copy-done.14, ...), custom_call_target="tpu_custom_call" | custom-call | flops 18790481920 | bytes 3145728 | tf_op jit(solution)/shard_map/agent_stage/pallas_call | solution.py:147
  176.0 2.1 collective-permute-start.21
  178.1 4.6 %collective-permute-done.19.refs_13_ = bf16[6,128,512]{2,1,0:T(8,128)(2,1)S(1)} collective-permute-done((bf16[6,128,512]{2,1,0:T(8,128)(2,1)S(1)}, bf16[6,128,512]{2,1,0:T(8,128)(2,1)S(1)}, u32[]{:S(2)}, u32[]{:S(2)}) %collective-permute-start.19) | collective-permute-done | bytes 786464 | tf_op jit(solution)/shard_map/ppermute | solution.py:629
  183.8 9.1 %agent_stage.7 = (f32[4,128,512]{2,1,0:T(8,128)S(1)}, bf16[4,128,512]{2,1,0:T(8,128)(2,1)}) custom-call(s32[32]{0:T(128)S(1)} %copy-done.13, bf16[16,128,512]{2,1,0:T(8,128)(2,1)S(1)} %copy-done.14, bf16[16,128,1536]{2,1,0:T(8,128)(2,1)S(1)} %own_stage.3.refs_6_.projected_ref, bf16[16,128,512]{2,1,0:T(8,128)(2,1)S(1)} %copy-done.14, ...), custom_call_target="tpu_custom_call" | custom-call | flops 18790481920 | bytes 3145728 | tf_op jit(solution)/shard_map/agent_stage/pallas_call | solution.py:147
  195.2 1.7 collective-permute-done.22.refs_5_
  199.4 16.4 %time_stage.3 = (f32[16,128]{1,0:T(8,128)}, f32[2,128]{1,0:T(2,128)S(1)}) custom-call(s32[1]{0:T(128)} %bitcast.13.offset_ref, f32[8,128,512]{2,1,0:T(8,128)S(1)} %copy-done.1, f32[4,128,512]{2,1,0:T(8,128)S(1)} %copy-done.5, f32[4,128,512]{2,1,0:T(8,128)S(1)} %copy-done.7, bf16[8,128,512]{2,1,0:T(8,128)(2,1)} %collective-permute-done.20.refs_3_, ...), custom_call_target="tpu_custom_call" | custom-call | bytes 256 | tf_op jit(solution)/shard_map/time_stage/pallas_call | solution.py:334
  219.3 1.4 advantage_stage.3
  (83 shorter events, 24.0 us)
Async XLA Ops:
  1.5 4.6 %collective-permute-start.2 = (s32[32]{0:T(128)S(1)}, s32[32]{0:T(128)S(1)}, u32[]{:S(2)}, u32[]{:S(2)}) collective-permute-start(s32[32]{0:T(128)S(1)} %reshape_squeeze.7), channel_id=1, source_target_pairs={{0,2},{2,0},{4,6},{6,4},{8,10},{10,8},{12,14},{14,12},{1,3},{3,1},... | collective-permute-start | bytes 392 | tf_op jit(solution)/shard_map/ppermute | solution.py:629
  6.0 5.3 %collective-permute-start.3 = (s32[2,32]{1,0:T(2,128)S(1)}, s32[2,32]{1,0:T(2,128)S(1)}, u32[]{:S(2)}, u32[]{:S(2)}) collective-permute-start(s32[2,32]{1,0:T(2,128)S(1)} %pad_add_fusion.1), channel_id=1, source_target_pairs={{0,4},{2,6},{12,8},{14,10},{1,5},{3,7},{13,9},{15,11},{16,20},{18,... | collective-permute-start | bytes 776 | tf_op jit(solution)/shard_map/ppermute | solution.py:629
  13.8 29.3 %collective-permute-start.4 = (bf16[8,128,512]{2,1,0:T(8,128)(2,1)}, bf16[8,128,512]{2,1,0:T(8,128)(2,1)S(1)}, u32[]{:S(2)}, u32[]{:S(2)}) collective-permute-start(bf16[8,128,512]{2,1,0:T(8,128)(2,1)} %constant_dynamic-slice_fusion), channel_id=1, source_target_pairs={{0,4},{2,6},{4,0},{6,2},{8,12},{10,14},{12,8},{14,10},{1,5},{3,7},... | collective-permute-start | bytes 3145736 | tf_op jit(solution)/shard_map/ppermute | solution.py:629
  16.1 27.0 %collective-permute-start.5 = (bf16[8,128,512]{2,1,0:T(8,128)(2,1)}, bf16[8,128,512]{2,1,0:T(8,128)(2,1)S(1)}, u32[]{:S(2)}, u32[]{:S(2)}) collective-permute-start(bf16[8,128,512]{2,1,0:T(8,128)(2,1)} %constant_dynamic-slice_fusion), channel_id=1, source_target_pairs={{4,8},{6,10},{8,4},{10,6},{5,9},{7,11},{9,5},{11,7},{20,24},{22,26... | collective-permute-start | bytes 3145736 | tf_op jit(solution)/shard_map/ppermute | solution.py:629
  28.4 14.7 %collective-permute-start.6 = (bf16[4,128,512]{2,1,0:T(8,128)(2,1)S(1)}, bf16[4,128,512]{2,1,0:T(8,128)(2,1)S(1)}, u32[]{:S(2)}, u32[]{:S(2)}) collective-permute-start(bf16[4,128,512]{2,1,0:T(8,128)(2,1)S(1)} %pack.6.refs_4_), channel_id=1, source_target_pairs={{0,2},{2,0},{4,6},{6,4},{8,10},{10,8},{12,14},{14,12},{1,3},{3,1},... | collective-permute-start | bytes 1572872 | tf_op jit(solution)/shard_map/ppermute | solution.py:629
  43.1 123.9 %copy-start.8 = (bf16[4,128,512]{2,1,0:T(8,128)(2,1)}, bf16[4,128,512]{2,1,0:T(8,128)(2,1)S(1)}, u32[]{:S(2)}) copy-start(bf16[4,128,512]{2,1,0:T(8,128)(2,1)S(1)} %collective-permute-done.6.refs_3_.refs_7_.refs_8_) | copy-start | bytes 1572868
  50.1 25.7 %collective-permute-start.7 = (bf16[8,128,512]{2,1,0:T(8,128)(2,1)S(1)}, bf16[8,128,512]{2,1,0:T(8,128)(2,1)S(1)}, u32[]{:S(2)}, u32[]{:S(2)}) collective-permute-start(bf16[8,128,512]{2,1,0:T(8,128)(2,1)S(1)} %get-tuple-element.72), channel_id=1, source_target_pairs={{0,4},{2,6},{4,0},{6,2},{8,12},{10,14},{12,8},{14,10},{1,5},{3,7},... | collective-permute-start | bytes 3145736 | tf_op jit(solution)/shard_map/ppermute | solution.py:629
  52.8 24.6 %copy-start.12 = (s32[77]{0:T(128)S(1)}, s32[77]{0:T(128)}, u32[]{:S(2)}) copy-start(s32[77]{0:T(128)} %get-tuple-element.70.table_ref) | copy-start | bytes 928
  52.8 24.6 %collective-permute-start.9 = (bf16[8,128,512]{2,1,0:T(8,128)(2,1)S(1)}, bf16[8,128,512]{2,1,0:T(8,128)(2,1)S(1)}, u32[]{:S(2)}, u32[]{:S(2)}) collective-permute-start(bf16[8,128,512]{2,1,0:T(8,128)(2,1)S(1)} %get-tuple-element.71.refs_0_), channel_id=1, source_target_pairs={{0,2},{2,0},{4,6},{6,4},{8,10},{10,8},{12,14},{14,12},{1,3},{3,1},... | collective-permute-start | bytes 3145736 | tf_op jit(solution)/shard_map/ppermute | solution.py:629
  53.2 24.1 %collective-permute-start.8 = (bf16[8,128,512]{2,1,0:T(8,128)(2,1)S(1)}, bf16[8,128,512]{2,1,0:T(8,128)(2,1)S(1)}, u32[]{:S(2)}, u32[]{:S(2)}) collective-permute-start(bf16[8,128,512]{2,1,0:T(8,128)(2,1)S(1)} %collective-permute-done.4.refs_1_), channel_id=1, source_target_pairs={{4,8},{6,10},{8,4},{10,6},{5,9},{7,11},{9,5},{11,7},{20,24},{22,26... | collective-permute-start | bytes 3145736 | tf_op jit(solution)/shard_map/ppermute | solution.py:629
  58.2 28.2 %collective-permute-start.11 = (bf16[8,128,512]{2,1,0:T(8,128)(2,1)S(1)}, bf16[8,128,512]{2,1,0:T(8,128)(2,1)S(1)}, u32[]{:S(2)}, u32[]{:S(2)}) collective-permute-start(bf16[8,128,512]{2,1,0:T(8,128)(2,1)S(1)} %get-tuple-element.74), channel_id=1, source_target_pairs={{4,8},{6,10},{8,4},{10,6},{5,9},{7,11},{9,5},{11,7},{20,24},{22,26... | collective-permute-start | bytes 3145736 | tf_op jit(solution)/shard_map/ppermute | solution.py:629
  80.6 25.4 %collective-permute-start.10 = (bf16[8,128,512]{2,1,0:T(8,128)(2,1)S(1)}, bf16[8,128,512]{2,1,0:T(8,128)(2,1)S(1)}, u32[]{:S(2)}, u32[]{:S(2)}) collective-permute-start(bf16[8,128,512]{2,1,0:T(8,128)(2,1)S(1)} %get-tuple-element.73), channel_id=1, source_target_pairs={{0,4},{2,6},{4,0},{6,2},{8,12},{10,14},{12,8},{14,10},{1,5},{3,7},... | collective-permute-start | bytes 3145736 | tf_op jit(solution)/shard_map/ppermute | solution.py:629
  85.6 21.9 %collective-permute-start.13 = (bf16[8,128,512]{2,1,0:T(8,128)(2,1)S(1)}, bf16[8,128,512]{2,1,0:T(8,128)(2,1)S(1)}, u32[]{:S(2)}, u32[]{:S(2)}) collective-permute-start(bf16[8,128,512]{2,1,0:T(8,128)(2,1)S(1)} %get-tuple-element.75.refs_9_), channel_id=1, source_target_pairs={{0,2},{2,0},{4,6},{6,4},{8,10},{10,8},{12,14},{14,12},{1,3},{3,1},... | collective-permute-start | bytes 3145736 | tf_op jit(solution)/shard_map/ppermute | solution.py:629
  85.7 0.7 collective-permute-start.12
  109.6 30.7 %collective-permute-start.14 = (bf16[8,128,512]{2,1,0:T(8,128)(2,1)S(1)}, bf16[8,128,512]{2,1,0:T(8,128)(2,1)S(1)}, u32[]{:S(2)}, u32[]{:S(2)}) collective-permute-start(bf16[8,128,512]{2,1,0:T(8,128)(2,1)S(1)} %get-tuple-element.76), channel_id=1, source_target_pairs={{0,4},{2,6},{4,0},{6,2},{8,12},{10,14},{12,8},{14,10},{1,5},{3,7},... | collective-permute-start | bytes 3145736 | tf_op jit(solution)/shard_map/ppermute | solution.py:629
  118.1 20.7 %collective-permute-start.15 = (bf16[7,128,512]{2,1,0:T(8,128)(2,1)S(1)}, bf16[7,128,512]{2,1,0:T(8,128)(2,1)S(1)}, u32[]{:S(2)}, u32[]{:S(2)}) collective-permute-start(bf16[7,128,512]{2,1,0:T(8,128)(2,1)S(1)} %get-tuple-element.77.refs_11_), channel_id=1, source_target_pairs={{0,2},{2,0},{4,6},{6,4},{8,10},{10,8},{12,14},{14,12},{1,3},{3,1},... | collective-permute-start | bytes 2752520 | tf_op jit(solution)/shard_map/ppermute | solution.py:629
  118.9 26.9 %copy-start.13 = (s32[32]{0:T(128)S(1)}, s32[32]{0:T(128)}, u32[]{:S(2)}) copy-start(s32[32]{0:T(128)} %get-tuple-element.69.table_ref) | copy-start | bytes 388
  118.9 26.9 %copy-start.27 = (bf16[512,512]{1,0:T(8,128)(2,1)S(1)}, bf16[512,512]{1,0:T(8,128)(2,1)}, u32[]{:S(2)}) copy-start(bf16[512,512]{1,0:T(8,128)(2,1)} %refs_16_.1) | copy-start | bytes 1572868
  118.9 0.8 collective-permute-start.16
  142.7 21.9 %collective-permute-start.17 = (bf16[6,128,512]{2,1,0:T(8,128)(2,1)S(1)}, bf16[6,128,512]{2,1,0:T(8,128)(2,1)S(1)}, u32[]{:S(2)}, u32[]{:S(2)}) collective-permute-start(bf16[6,128,512]{2,1,0:T(8,128)(2,1)S(1)} %get-tuple-element.80), channel_id=1, source_target_pairs={{0,4},{2,6},{4,0},{6,2},{8,12},{10,14},{12,8},{14,10},{1,5},{3,7},... | collective-permute-start | bytes 2359304 | tf_op jit(solution)/shard_map/ppermute | solution.py:629
  144.5 20.1 %collective-permute-start.18 = (bf16[6,128,512]{2,1,0:T(8,128)(2,1)S(1)}, bf16[6,128,512]{2,1,0:T(8,128)(2,1)S(1)}, u32[]{:S(2)}, u32[]{:S(2)}) collective-permute-start(bf16[6,128,512]{2,1,0:T(8,128)(2,1)S(1)} %get-tuple-element.78.refs_11_), channel_id=1, source_target_pairs={{0,2},{2,0},{4,6},{6,4},{8,10},{10,8},{12,14},{14,12},{1,3},{3,1},... | collective-permute-start | bytes 2359304 | tf_op jit(solution)/shard_map/ppermute | solution.py:629
  162.3 32.9 %collective-permute-start.20 = (bf16[8,128,512]{2,1,0:T(8,128)(2,1)}, bf16[8,128,512]{2,1,0:T(8,128)(2,1)}, u32[]{:S(2)}, u32[]{:S(2)}) collective-permute-start(bf16[8,128,512]{2,1,0:T(8,128)(2,1)} %get-tuple-element.83), channel_id=1, source_target_pairs={{0,1},{2,3},{4,5},{6,7},{8,9},{10,11},{12,13},{14,15},{16,17},{18,... | collective-permute-start | bytes 3145736 | tf_op jit(solution)/shard_map/ppermute | solution.py:748
  166.1 16.6 %collective-permute-start.19 = (bf16[6,128,512]{2,1,0:T(8,128)(2,1)S(1)}, bf16[6,128,512]{2,1,0:T(8,128)(2,1)S(1)}, u32[]{:S(2)}, u32[]{:S(2)}) collective-permute-start(bf16[6,128,512]{2,1,0:T(8,128)(2,1)S(1)} %pack.11.refs_13_), channel_id=1, source_target_pairs={{0,2},{2,0},{4,6},{6,4},{8,10},{10,8},{12,14},{14,12},{1,3},{3,1},... | collective-permute-start | bytes 2359304 | tf_op jit(solution)/shard_map/ppermute | solution.py:629
  176.0 16.9 %copy-start.4 = (f32[4,128,512]{2,1,0:T(8,128)}, f32[4,128,512]{2,1,0:T(8,128)S(1)}, u32[]{:S(2)}) copy-start(f32[4,128,512]{2,1,0:T(8,128)S(1)} %get-tuple-element.81.refs_14_.refs_1_) | copy-start | bytes 3145732
  176.0 19.2 %collective-permute-start.21 = (bf16[4,128,512]{2,1,0:T(8,128)(2,1)}, bf16[4,128,512]{2,1,0:T(8,128)(2,1)}, u32[]{:S(2)}, u32[]{:S(2)}) collective-permute-start(bf16[4,128,512]{2,1,0:T(8,128)(2,1)} %get-tuple-element.84), channel_id=1, source_target_pairs={{0,1},{2,3},{4,5},{6,7},{8,9},{10,11},{12,13},{14,15},{16,17},{18,... | collective-permute-start | bytes 1572872 | tf_op jit(solution)/shard_map/ppermute | solution.py:748
  183.7 13.2 %copy-start.19 = (s32[16,128]{1,0:T(8,128)S(1)}, s32[16,128]{1,0:T(8,128)}, u32[]{:S(2)}) copy-start(s32[16,128]{1,0:T(8,128)} %done_ref.1) | copy-start | bytes 24580
  183.7 13.2 %copy-start.20 = (f32[16,128]{1,0:T(8,128)S(1)}, f32[16,128]{1,0:T(8,128)}, u32[]{:S(2)}) copy-start(f32[16,128]{1,0:T(8,128)} %rewards_ref.1) | copy-start | bytes 24580
  183.7 13.2 %copy-start.21 = (f32[512]{0:T(512)S(1)}, f32[512]{0:T(512)}, u32[]{:S(2)}) copy-start(f32[512]{0:T(512)} %param.21) | copy-start | bytes 6148
  183.8 13.2 %copy-start.22 = (f32[128]{0:T(128)S(1)}, f32[128]{0:T(128)}, u32[]{:S(2)}) copy-start(f32[128]{0:T(128)} %param.16) | copy-start | bytes 1540
  193.9 3.0 %collective-permute-start.22 = (bf16[4,128,512]{2,1,0:T(8,128)(2,1)}, bf16[4,128,512]{2,1,0:T(8,128)(2,1)S(1)}, u32[]{:S(2)}, u32[]{:S(2)}) collective-permute-start(bf16[4,128,512]{2,1,0:T(8,128)(2,1)} %get-tuple-element.85), channel_id=1, source_target_pairs={{0,1},{2,3},{4,5},{6,7},{8,9},{10,11},{12,13},{14,15},{16,17},{18,... | collective-permute-start | bytes 1572872 | tf_op jit(solution)/shard_map/ppermute | solution.py:748
  199.4 21.3 %copy-start.23 = (s32[1,16,2]{1,2,0:T(2,128)S(1)}, s32[1,16,2]{1,2,0:T(2,128)}, u32[]{:S(2)}) copy-start(s32[1,16,2]{1,2,0:T(2,128)} %param.13) | copy-start | bytes 388
  215.8 3.0 %collective-permute-start.23 = (f32[2,128]{1,0:T(2,128)S(1)}, f32[2,128]{1,0:T(2,128)S(1)}, u32[]{:S(2)}, u32[]{:S(2)}) collective-permute-start(f32[2,128]{1,0:T(2,128)S(1)} %get-tuple-element.87), channel_id=1, source_target_pairs={{1,0},{3,2},{5,4},{7,6},{9,8},{11,10},{13,12},{15,14},{17,16},{19,... | collective-permute-start | bytes 3080 | tf_op jit(solution)/shard_map/ppermute | solution.py:765
  (12 other events, 49.7 us)

commit v2 on v1

--- a/solution.py
+++ b/solution.py
@@ -65,15 +65,16 @@
             pltpu.make_async_copy(ref.at[entry % SPAN], target, sem).start()
 
 
-def own_kernel(idle, own_ref, proj_ref, *refs):
-    projected_ref = refs[idle]
+def own_kernel(idle, own_ref, proj_ref, flag_ref, *refs):
+    projected_ref, tile_ref = refs[idle:]
+    tile_ref[...] = jnp.full(tile_ref.shape, flag_ref[0], jnp.int32)
     together, agents, width = own_ref.shape
     mine = rms(own_ref[...].astype(f32).reshape(together * agents, width)).astype(bf16)
     projected = dot(mine, proj_ref[...]).astype(bf16)
     projected_ref[...] = projected.reshape(together, agents, proj_ref.shape[1])
 
 
-def own_stage(embedded, proj, after=()):
+def own_stage(embedded, proj, flag, after=()):
     steps, agents, width = embedded.shape
     together = math.gcd(steps, 4)
     return pl.pallas_call(
@@ -82,13 +83,20 @@
         in_specs=[
             pl.BlockSpec((together, agents, width), lambda i: (i, 0, 0)),
             pl.BlockSpec(proj.shape, lambda i: (0, 0)),
+            pl.BlockSpec(memory_space=pltpu.SMEM),
         ]
         + [pl.BlockSpec(memory_space=pltpu.HBM)] * len(after),
-        out_specs=pl.BlockSpec((together, agents, proj.shape[1]), lambda i: (i, 0, 0)),
-        out_shape=jax.ShapeDtypeStruct((steps, agents, proj.shape[1]), bf16),
+        out_specs=[
+            pl.BlockSpec((together, agents, proj.shape[1]), lambda i: (i, 0, 0)),
+            pl.BlockSpec((8, 128), lambda i: (0, 0)),
+        ],
+        out_shape=[
+            jax.ShapeDtypeStruct((steps, agents, proj.shape[1]), bf16),
+            jax.ShapeDtypeStruct((8, 128), jnp.int32),
+        ],
         compiler_params=pltpu.CompilerParams(vmem_limit_bytes=18 * MIB),
         name="own_stage",
-    )(embedded, proj, *after)
+    )(embedded, proj, flag, *after)
 
 
 def agent_kernel(
@@ -643,8 +651,6 @@
         parts = [across_part(n)]
         if n < len(outward):
             parts.append((e_base[n], outward[n], None))
-        if n == 1:
-            parts.append((None, outward[1], starts[1]))
         after = tuple(arrays[rows[b]] for b in settled) + tuple(after)
         packed = pack(out_table, pick([own] + reads), parts, after)
         if n < len(outward):
@@ -669,17 +675,18 @@
     )
     (token,) = pack(out_table, pick([own]), [across_part(0)])
     arrays[rows[0]] = send(token, over)
-    crowded = jnp.max(shared(flag, ("groups", "agent", "tm")))
     arrays[far[0]] = send(arrays[edge[0]], swap)
     reads = edge[:1] + swapped[:1]
-    packed = stage(1, reads, (0,), (token, crowded.reshape(1)))
-    arrays[swapped[1]] = send(packed[2], swap)
+    packed = stage(1, reads, (0,), (token,))
+    projected, tile = own_projection(flag, packed[:1])
+    crowded = jnp.max(shared(tile[0, :1], ("groups", "agent", "tm")))
+    (second,) = pack(out_table, pick([own]), [(None, outward[1], starts[1])], (crowded.reshape(1),))
+    arrays[swapped[1]] = send(second, swap)
     for k in (1, 2):
         at = starts[k] - starts[1]
         arrays[far[k]] = send(arrays[edge[1]][at : at + chunks[k]], swap)
     reads = reads + edge[1:2] + far[:1]
-    projected = own_projection(packed[:1])
-    packed = stage(2, reads, (1,), (projected,))
+    packed = stage(2, reads, (1,), (second,))
     reads = reads + edge[2:3] + swapped[1:] + far[1:2]
     packed = stage(3, reads, (2,), packed[:1])
     reads = reads + edge[3:4] + far[2:3]
@@ -729,8 +736,8 @@
     forward = [(i, i + 1) for i in range(spans - 1)]
     backward = [(i + 1, i) for i in range(spans - 1)]
 
-    def own_projection(after=()):
-        return own_stage(embedded, agent_proj, after)
+    def own_projection(flag, after=()):
+        return own_stage(embedded, agent_proj, flag, after)
 
     def attention(first, count, arrays, table, projected, after=()):
         residual, normed = agent_stage(
@@ -768,7 +775,7 @@
 
     def padded():
         pool, where = exchange_slots(embedded, lists, capacity)
-        return finish([attention(0, steps, {1: pool}, where + SPAN, own_projection())])
+        return finish([attention(0, steps, {1: pool}, where + SPAN, own_projection(offset)[0])])
 
     if blocks != COLUMNS * ROWS or steps % 4:
         return padded()

time: 222 us -> 223 us (level)
  waiting for transfers between devices: 70.1 us -> 62.4 us
  starting transfers between devices: 42.5 us -> 45.6 us
  local copies, waits for them, and re-layouts: 10.4 us -> 13 us
    ppermute x18, waiting for transfers between devices: 67.4 us -> 59.7 us  [relay(): send = lambda value, pairs: lax.ppermute(value, 'agent', pairs)]
    ppermute x18, starting transfers between devices: 35.5 us -> 38.6 us  [relay(): send = lambda value, pairs: lax.ppermute(value, 'agent', pairs)]
    unnamed x45 -> x53, local copies, waits for them, and re-layouts: 7.18 us -> 9.21 us
    pallas_call x6 -> x7, Pallas kernels: 17.8 us -> 19.6 us  [pack(): pl.pallas_call(functools.partial(pack_kernel, tuple(arrays), tuple(parts)...]
  transfers between devices with their start and end apart: 22 -> 22, of which waited for: 11 -> 10; matrix products, arithmetic and copies ran while one was open for 1% -> 1% of each run, Pallas kernels for 24% -> 26%
where the time goes in v2:
time: 223 us; the launch traced here: 221 us
  Pallas kernels  84.5 us (38%)
  waiting for transfers between devices  62.4 us (28%)
  starting transfers between devices  45.6 us (20%)
  local copies, waits for them, and re-layouts  13 us (6%)
  blocking collectives  12.6 us (6%)
    ppermute x18, waiting for transfers between devices, relay(): send = lambda value, pairs: lax.ppermute(value, 'agent', pairs)  59.7 us
    ppermute x18, starting transfers between devices, relay(): send = lambda value, pairs: lax.ppermute(value, 'agent', pairs)  38.6 us
    pallas_call x3, Pallas kernels, agent_stage(): pl.pallas_call(functools.partial(agent_kernel, list_length, first_step, t...  34.2 us
    pallas_call x7, Pallas kernels, pack(): pl.pallas_call(functools.partial(pack_kernel, tuple(arrays), tuple(parts)...  19.6 us
    pallas_call x1, Pallas kernels, time_stage(): pl.pallas_call(functools.partial(time_kernel, len(residuals), steps, tile...  16.4 us
    all_to_all x1, blocking collectives, shared(): return lax.all_to_all(rows, axes, split_axis=0, concat_axis=0, tiled=True)  12.6 us
    unnamed x53, local copies, waits for them, and re-layouts  9.21 us
    pallas_call x1, Pallas kernels, plan(): pl.pallas_call(functools.partial(plan_kernel, steps, list_length, chunks,...  8.07 us
  transfers between devices with their start and end apart: 22, of which 10 were waited for; matrix products, arithmetic and copies ran while one was open for 1% of the time, Pallas kernels for 26%

profile of v2, /device:TPU:0, one launch (start us, length us, event | category | flops | bytes accessed | tf_op | source)
XLA Modules:
  0.0 221.4 jit_solution(4392723760758967330)
XLA Ops:
  1.5 3.0 %collective-permute-start.2 = (s32[32]{0:T(128)S(1)}, s32[32]{0:T(128)S(1)}, u32[]{:S(2)}, u32[]{:S(2)}) collective-permute-start(s32[32]{0:T(128)S(1)} %reshape_squeeze.7), channel_id=1, source_target_pairs={{0,2},{2,0},{4,6},{6,4},{8,10},{10,8},{12,14},{14,12},{1,3},{3,1},... | collective-permute-start | bytes 392 | tf_op jit(solution)/shard_map/ppermute | solution.py:637
  6.0 4.0 %collective-permute-start.3 = (s32[2,32]{1,0:T(2,128)S(1)}, s32[2,32]{1,0:T(2,128)S(1)}, u32[]{:S(2)}, u32[]{:S(2)}) collective-permute-start(s32[2,32]{1,0:T(2,128)S(1)} %pad_add_fusion.1), channel_id=1, source_target_pairs={{0,4},{2,6},{12,8},{14,10},{1,5},{3,7},{13,9},{15,11},{16,20},{18,... | collective-permute-start | bytes 776 | tf_op jit(solution)/shard_map/ppermute | solution.py:637
  11.5 2.3 %constant_dynamic-slice_fusion = bf16[8,128,512]{2,1,0:T(8,128)(2,1)} fusion(bf16[16,128,512]{2,1,0:T(8,128)(2,1)} %refs_0_.19, s32[]{:T(128)S(6)} %select_n.68), kind=kLoop, calls=%fused_computation.24 | loop fusion | bytes 2097156 | tf_op jit(solution)/shard_map/dynamic_slice | solution.py:670
  13.8 2.3 %collective-permute-start.4 = (bf16[8,128,512]{2,1,0:T(8,128)(2,1)}, bf16[8,128,512]{2,1,0:T(8,128)(2,1)S(1)}, u32[]{:S(2)}, u32[]{:S(2)}) collective-permute-start(bf16[8,128,512]{2,1,0:T(8,128)(2,1)} %constant_dynamic-slice_fusion), channel_id=1, source_target_pairs={{0,4},{2,6},{4,0},{6,2},{8,12},{10,14},{12,8},{14,10},{1,5},{3,7},... | collective-permute-start | bytes 3145736 | tf_op jit(solution)/shard_map/ppermute | solution.py:637
  17.4 8.1 %plan.1 = (s32[77]{0:T(128)}, s32[32]{0:T(128)}, s32[1]{0:T(128)}) custom-call(s32[2]{0:T(128)} %pad_add_fusion.2.place_ref, s32[128]{0:T(128)} %copy-done.27), custom_call_target="tpu_custom_call" | custom-call | tf_op jit(solution)/shard_map/plan/pallas_call | solution.py:599
  26.1 2.0 pack.7.refs_4_
  28.1 1.8 collective-permute-start.6
  29.8 9.5 %collective-permute-done.6.refs_3_.refs_7_.refs_8_ = bf16[4,128,512]{2,1,0:T(8,128)(2,1)S(1)} collective-permute-done((bf16[4,128,512]{2,1,0:T(8,128)(2,1)S(1)}, bf16[4,128,512]{2,1,0:T(8,128)(2,1)S(1)}, u32[]{:S(2)}, u32[]{:S(2)}) %collective-permute-start.6) | collective-permute-done | bytes 524320 | tf_op jit(solution)/shard_map/ppermute | solution.py:637
  40.0 3.0 %pack.8 = (bf16[8,128,512]{2,1,0:T(8,128)(2,1)}, bf16[8,128,512]{2,1,0:T(8,128)(2,1)}) custom-call(s32[77]{0:T(128)S(1)} %copy-done.7, bf16[16,128,512]{2,1,0:T(8,128)(2,1)} %refs_0_.19, bf16[8,128,512]{2,1,0:T(8,128)(2,1)S(1)} %collective-permute-done.4.refs_1_, bf16[8,128,512]{2,1,0:T(8,128)(2,1)S(1)} %collective-permute-done.5.refs_2_.refs_5_, ...), custom_call_target="tpu_custom_call" | custom-call | bytes 65536 | tf_op jit(solution)/shard_map/pack/pallas_call | solution.py:227
  43.0 4.2 %collective-permute-start.7 = (bf16[8,128,512]{2,1,0:T(8,128)(2,1)}, bf16[8,128,512]{2,1,0:T(8,128)(2,1)S(1)}, u32[]{:S(2)}, u32[]{:S(2)}) collective-permute-start(bf16[8,128,512]{2,1,0:T(8,128)(2,1)} %get-tuple-element.76), channel_id=1, source_target_pairs={{0,4},{2,6},{4,0},{6,2},{8,12},{10,14},{12,8},{14,10},{1,5},{3,7},... | collective-permute-start | bytes 3145736 | tf_op jit(solution)/shard_map/ppermute | solution.py:637
  47.2 1.7 collective-permute-start.9
  48.9 1.7 collective-permute-start.8
  50.6 4.9 %own_stage.3 = (bf16[16,128,1536]{2,1,0:T(8,128)(2,1)S(1)}, s32[8,128]{1,0:T(8,128)S(1)}) custom-call(bf16[16,128,512]{2,1,0:T(8,128)(2,1)S(1)} %copy-done.13, bf16[512,1536]{1,0:T(8,128)(2,1)S(1)} %copy-done.17, s32[1]{0:T(128)} %get-tuple-element.70.flag_ref, bf16[8,128,512]{2,1,0:T(8,128)(2,1)} %get-tuple-element.72.refs_0_), custom_call_target="tpu_custom_call" | custom-call | tf_op jit(solution)/shard_map/own_stage/pallas_call | solution.py:80
  55.5 2.6 %copy-done.9 = bf16[16,128,1536]{2,1,0:T(8,128)(2,1)} copy-done((bf16[16,128,1536]{2,1,0:T(8,128)(2,1)}, bf16[16,128,1536]{2,1,0:T(8,128)(2,1)S(1)}, u32[]{:S(2)}) %copy-start.9) | copy-done | bytes 6291480
  59.4 12.6 %all_to_all.18 = s32[32,1,1]{2,1,0:T(1,128)S(1)} all-to-all(s32[32,1,1]{2,1,0:T(1,128)S(1)} %broadcast_in_dim.5), channel_id=1, replica_groups=mesh['groups'=2,'agent'=8,'tm'=2] {'groups','agent','tm'}, dimensions={0} | all-to-all | bytes 256 | tf_op jit(solution)/shard_map/all_to_all | solution.py:620
  72.7 3.7 %pack.9.refs_6_ = bf16[8,128,512]{2,1,0:T(8,128)(2,1)S(1)} custom-call(s32[77]{0:T(128)S(1)} %copy-done.8, bf16[16,128,512]{2,1,0:T(8,128)(2,1)} %refs_0_.19, s32[1]{0:T(128)} %bitcast.15.refs_1_), custom_call_target="tpu_custom_call" | custom-call | bytes 65536 | tf_op jit(solution)/shard_map/pack/pallas_call | solution.py:227
  77.2 3.2 %pack.10 = (bf16[8,128,512]{2,1,0:T(8,128)(2,1)S(1)}, bf16[8,128,512]{2,1,0:T(8,128)(2,1)S(1)}) custom-call(s32[77]{0:T(128)S(1)} %copy-done.8, bf16[16,128,512]{2,1,0:T(8,128)(2,1)S(1)} %copy-done.14, bf16[8,128,512]{2,1,0:T(8,128)(2,1)S(1)} %collective-permute-done.4.refs_1_, bf16[8,128,512]{2,1,0:T(8,128)(2,1)S(1)} %collective-permute-done.5.refs_2_.refs_5_, ...), custom_call_target="tpu_custom_call" | custom-call | bytes 65536 | tf_op jit(solution)/shard_map/pack/pallas_call | solution.py:227
  80.4 2.9 %collective-permute-start.10 = (bf16[8,128,512]{2,1,0:T(8,128)(2,1)S(1)}, bf16[8,128,512]{2,1,0:T(8,128)(2,1)S(1)}, u32[]{:S(2)}, u32[]{:S(2)}) collective-permute-start(bf16[8,128,512]{2,1,0:T(8,128)(2,1)S(1)} %get-tuple-element.77), channel_id=1, source_target_pairs={{0,4},{2,6},{4,0},{6,2},{8,12},{10,14},{12,8},{14,10},{1,5},{3,7},... | collective-permute-start | bytes 3145736 | tf_op jit(solution)/shard_map/ppermute | solution.py:637
  84.3 22.4 %collective-permute-done.10.refs_5_.refs_3_ = bf16[8,128,512]{2,1,0:T(8,128)(2,1)S(1)} collective-permute-done((bf16[8,128,512]{2,1,0:T(8,128)(2,1)S(1)}, bf16[8,128,512]{2,1,0:T(8,128)(2,1)S(1)}, u32[]{:S(2)}, u32[]{:S(2)}) %collective-permute-start.10) | collective-permute-done | bytes 1048608 | tf_op jit(solution)/shard_map/ppermute | solution.py:637
  108.2 3.0 %pack.11 = (bf16[7,128,512]{2,1,0:T(8,128)(2,1)S(1)}, bf16[8,128,512]{2,1,0:T(8,128)(2,1)S(1)}) custom-call(s32[77]{0:T(128)S(1)} %copy-done.8, bf16[16,128,512]{2,1,0:T(8,128)(2,1)S(1)} %copy-done.14, bf16[8,128,512]{2,1,0:T(8,128)(2,1)S(1)} %collective-permute-done.4.refs_1_, bf16[8,128,512]{2,1,0:T(8,128)(2,1)S(1)} %collective-permute-done.5.refs_2_.refs_5_, ...), custom_call_target="tpu_custom_call" | custom-call | bytes 65536 | tf_op jit(solution)/shard_map/pack/pallas_call | solution.py:227
  111.2 9.6 %collective-permute-start.14 = (bf16[8,128,512]{2,1,0:T(8,128)(2,1)S(1)}, bf16[8,128,512]{2,1,0:T(8,128)(2,1)S(1)}, u32[]{:S(2)}, u32[]{:S(2)}) collective-permute-start(bf16[8,128,512]{2,1,0:T(8,128)(2,1)S(1)} %get-tuple-element.79), channel_id=1, source_target_pairs={{0,4},{2,6},{4,0},{6,2},{8,12},{10,14},{12,8},{14,10},{1,5},{3,7},... | collective-permute-start | bytes 3145736 | tf_op jit(solution)/shard_map/ppermute | solution.py:637
  121.7 19.4 %collective-permute-done.15.refs_10_.refs_11_ = bf16[7,128,512]{2,1,0:T(8,128)(2,1)S(1)} collective-permute-done((bf16[7,128,512]{2,1,0:T(8,128)(2,1)S(1)}, bf16[7,128,512]{2,1,0:T(8,128)(2,1)S(1)}, u32[]{:S(2)}, u32[]{:S(2)}) %collective-permute-start.15) | collective-permute-done | bytes 917536 | tf_op jit(solution)/shard_map/ppermute | solution.py:637
  142.4 3.6 %pack.12 = (bf16[6,128,512]{2,1,0:T(8,128)(2,1)S(1)}, bf16[6,128,512]{2,1,0:T(8,128)(2,1)S(1)}) custom-call(s32[77]{0:T(128)S(1)} %copy-done.8, bf16[16,128,512]{2,1,0:T(8,128)(2,1)S(1)} %copy-done.14, bf16[8,128,512]{2,1,0:T(8,128)(2,1)S(1)} %collective-permute-done.4.refs_1_, bf16[8,128,512]{2,1,0:T(8,128)(2,1)S(1)} %collective-permute-done.5.refs_2_.refs_5_, ...), custom_call_target="tpu_custom_call" | custom-call | bytes 65536 | tf_op jit(solution)/shard_map/pack/pallas_call | solution.py:227
  147.6 16.1 %agent_stage.5 = (f32[8,128,512]{2,1,0:T(8,128)S(1)}, bf16[8,128,512]{2,1,0:T(8,128)(2,1)}) custom-call(s32[32]{0:T(128)S(1)} %copy-done.12, bf16[16,128,512]{2,1,0:T(8,128)(2,1)S(1)} %copy-done.14, bf16[16,128,1536]{2,1,0:T(8,128)(2,1)S(1)} %bitcast.24, bf16[16,128,512]{2,1,0:T(8,128)(2,1)S(1)} %copy-done.14, ...), custom_call_target="tpu_custom_call" | custom-call | flops 37580963840 | bytes 6291456 | tf_op jit(solution)/shard_map/agent_stage/pallas_call | solution.py:155
  163.6 2.3 %collective-permute-start.20 = (bf16[8,128,512]{2,1,0:T(8,128)(2,1)}, bf16[8,128,512]{2,1,0:T(8,128)(2,1)}, u32[]{:S(2)}, u32[]{:S(2)}) collective-permute-start(bf16[8,128,512]{2,1,0:T(8,128)(2,1)} %get-tuple-element.86), channel_id=1, source_target_pairs={{0,1},{2,3},{4,5},{6,7},{8,9},{10,11},{12,13},{14,15},{16,17},{18,... | collective-permute-start | bytes 3145736 | tf_op jit(solution)/shard_map/ppermute | solution.py:755
  167.0 2.9 %collective-permute-start.19 = (bf16[6,128,512]{2,1,0:T(8,128)(2,1)S(1)}, bf16[6,128,512]{2,1,0:T(8,128)(2,1)S(1)}, u32[]{:S(2)}, u32[]{:S(2)}) collective-permute-start(bf16[6,128,512]{2,1,0:T(8,128)(2,1)S(1)} %pack.13.refs_13_), channel_id=1, source_target_pairs={{0,2},{2,0},{4,6},{6,4},{8,10},{10,8},{12,14},{14,12},{1,3},{3,1},... | collective-permute-start | bytes 2359304 | tf_op jit(solution)/shard_map/ppermute | solution.py:637
  170.0 9.1 %agent_stage.6 = (f32[4,128,512]{2,1,0:T(8,128)S(1)}, bf16[4,128,512]{2,1,0:T(8,128)(2,1)}) custom-call(s32[32]{0:T(128)S(1)} %copy-done.12, bf16[16,128,512]{2,1,0:T(8,128)(2,1)S(1)} %copy-done.14, bf16[16,128,1536]{2,1,0:T(8,128)(2,1)S(1)} %bitcast.24, bf16[16,128,512]{2,1,0:T(8,128)(2,1)S(1)} %copy-done.14, ...), custom_call_target="tpu_custom_call" | custom-call | flops 18790481920 | bytes 3145728 | tf_op jit(solution)/shard_map/agent_stage/pallas_call | solution.py:155
  179.0 2.1 collective-permute-start.21
  181.1 2.8 %collective-permute-done.19.refs_13_ = bf16[6,128,512]{2,1,0:T(8,128)(2,1)S(1)} collective-permute-done((bf16[6,128,512]{2,1,0:T(8,128)(2,1)S(1)}, bf16[6,128,512]{2,1,0:T(8,128)(2,1)S(1)}, u32[]{:S(2)}, u32[]{:S(2)}) %collective-permute-start.19) | collective-permute-done | bytes 786464 | tf_op jit(solution)/shard_map/ppermute | solution.py:637
  183.9 9.1 %agent_stage.7 = (f32[4,128,512]{2,1,0:T(8,128)S(1)}, bf16[4,128,512]{2,1,0:T(8,128)(2,1)}) custom-call(s32[32]{0:T(128)S(1)} %copy-done.12, bf16[16,128,512]{2,1,0:T(8,128)(2,1)S(1)} %copy-done.14, bf16[16,128,1536]{2,1,0:T(8,128)(2,1)S(1)} %bitcast.24, bf16[16,128,512]{2,1,0:T(8,128)(2,1)S(1)} %copy-done.14, ...), custom_call_target="tpu_custom_call" | custom-call | flops 18790481920 | bytes 3145728 | tf_op jit(solution)/shard_map/agent_stage/pallas_call | solution.py:155
  195.4 1.7 collective-permute-done.22.refs_5_
  199.9 16.4 %time_stage.3 = (f32[16,128]{1,0:T(8,128)}, f32[2,128]{1,0:T(2,128)S(1)}) custom-call(s32[1]{0:T(128)} %bitcast.14.offset_ref, f32[8,128,512]{2,1,0:T(8,128)S(1)} %copy-done.1, f32[4,128,512]{2,1,0:T(8,128)S(1)} %get-tuple-element.84.refs_14_.refs_1_, f32[4,128,512]{2,1,0:T(8,128)S(1)} %copy-done.3, bf16[8,128,512]{2,1,0:T(8,128)(2,1)} %collective-permute-done.20.refs_3_, ...), custom_call_target="tpu_custom_call" | custom-call | bytes 256 | tf_op jit(solution)/shard_map/time_stage/pallas_call | solution.py:342
  (94 shorter events, 25.8 us)
Async XLA Ops:
  1.5 4.6 %collective-permute-start.2 = (s32[32]{0:T(128)S(1)}, s32[32]{0:T(128)S(1)}, u32[]{:S(2)}, u32[]{:S(2)}) collective-permute-start(s32[32]{0:T(128)S(1)} %reshape_squeeze.7), channel_id=1, source_target_pairs={{0,2},{2,0},{4,6},{6,4},{8,10},{10,8},{12,14},{14,12},{1,3},{3,1},... | collective-permute-start | bytes 392 | tf_op jit(solution)/shard_map/ppermute | solution.py:637
  6.0 5.3 %collective-permute-start.3 = (s32[2,32]{1,0:T(2,128)S(1)}, s32[2,32]{1,0:T(2,128)S(1)}, u32[]{:S(2)}, u32[]{:S(2)}) collective-permute-start(s32[2,32]{1,0:T(2,128)S(1)} %pad_add_fusion.1), channel_id=1, source_target_pairs={{0,4},{2,6},{12,8},{14,10},{1,5},{3,7},{13,9},{15,11},{16,20},{18,... | collective-permute-start | bytes 776 | tf_op jit(solution)/shard_map/ppermute | solution.py:637
  13.8 25.5 %collective-permute-start.4 = (bf16[8,128,512]{2,1,0:T(8,128)(2,1)}, bf16[8,128,512]{2,1,0:T(8,128)(2,1)S(1)}, u32[]{:S(2)}, u32[]{:S(2)}) collective-permute-start(bf16[8,128,512]{2,1,0:T(8,128)(2,1)} %constant_dynamic-slice_fusion), channel_id=1, source_target_pairs={{0,4},{2,6},{4,0},{6,2},{8,12},{10,14},{12,8},{14,10},{1,5},{3,7},... | collective-permute-start | bytes 3145736 | tf_op jit(solution)/shard_map/ppermute | solution.py:637
  16.1 23.3 %collective-permute-start.5 = (bf16[8,128,512]{2,1,0:T(8,128)(2,1)}, bf16[8,128,512]{2,1,0:T(8,128)(2,1)S(1)}, u32[]{:S(2)}, u32[]{:S(2)}) collective-permute-start(bf16[8,128,512]{2,1,0:T(8,128)(2,1)} %constant_dynamic-slice_fusion), channel_id=1, source_target_pairs={{4,8},{6,10},{8,4},{10,6},{5,9},{7,11},{9,5},{11,7},{20,24},{22,26... | collective-permute-start | bytes 3145736 | tf_op jit(solution)/shard_map/ppermute | solution.py:637
  26.1 24.5 %copy-start.13 = (bf16[16,128,512]{2,1,0:T(8,128)(2,1)S(1)}, bf16[16,128,512]{2,1,0:T(8,128)(2,1)}, u32[]{:S(2)}) copy-start(bf16[16,128,512]{2,1,0:T(8,128)(2,1)} %refs_0_.19) | copy-start | bytes 6291460
  26.1 46.6 %copy-start.8 = (s32[77]{0:T(128)S(1)}, s32[77]{0:T(128)}, u32[]{:S(2)}) copy-start(s32[77]{0:T(128)} %get-tuple-element.71.table_ref) | copy-start | bytes 928
  28.1 11.3 %collective-permute-start.6 = (bf16[4,128,512]{2,1,0:T(8,128)(2,1)S(1)}, bf16[4,128,512]{2,1,0:T(8,128)(2,1)S(1)}, u32[]{:S(2)}, u32[]{:S(2)}) collective-permute-start(bf16[4,128,512]{2,1,0:T(8,128)(2,1)S(1)} %pack.7.refs_4_), channel_id=1, source_target_pairs={{0,2},{2,0},{4,6},{6,4},{8,10},{10,8},{12,14},{14,12},{1,3},{3,1},... | collective-permute-start | bytes 1572872 | tf_op jit(solution)/shard_map/ppermute | solution.py:637
  43.0 34.1 %collective-permute-start.7 = (bf16[8,128,512]{2,1,0:T(8,128)(2,1)}, bf16[8,128,512]{2,1,0:T(8,128)(2,1)S(1)}, u32[]{:S(2)}, u32[]{:S(2)}) collective-permute-start(bf16[8,128,512]{2,1,0:T(8,128)(2,1)} %get-tuple-element.76), channel_id=1, source_target_pairs={{0,4},{2,6},{4,0},{6,2},{8,12},{10,14},{12,8},{14,10},{1,5},{3,7},... | collective-permute-start | bytes 3145736 | tf_op jit(solution)/shard_map/ppermute | solution.py:637
  47.2 30.0 %collective-permute-start.9 = (bf16[8,128,512]{2,1,0:T(8,128)(2,1)}, bf16[8,128,512]{2,1,0:T(8,128)(2,1)}, u32[]{:S(2)}, u32[]{:S(2)}) collective-permute-start(bf16[8,128,512]{2,1,0:T(8,128)(2,1)} %get-tuple-element.72.refs_0_), channel_id=1, source_target_pairs={{0,2},{2,0},{4,6},{6,4},{8,10},{10,8},{12,14},{14,12},{1,3},{3,1},... | collective-permute-start | bytes 3145736 | tf_op jit(solution)/shard_map/ppermute | solution.py:637
  48.9 28.3 %collective-permute-start.8 = (bf16[8,128,512]{2,1,0:T(8,128)(2,1)S(1)}, bf16[8,128,512]{2,1,0:T(8,128)(2,1)}, u32[]{:S(2)}, u32[]{:S(2)}) collective-permute-start(bf16[8,128,512]{2,1,0:T(8,128)(2,1)S(1)} %collective-permute-done.4.refs_1_), channel_id=1, source_target_pairs={{4,8},{6,10},{8,4},{10,6},{5,9},{7,11},{9,5},{11,7},{20,24},{22,26... | collective-permute-start | bytes 3145736 | tf_op jit(solution)/shard_map/ppermute | solution.py:637
  76.4 7.9 %collective-permute-start.11 = (bf16[8,128,512]{2,1,0:T(8,128)(2,1)S(1)}, bf16[8,128,512]{2,1,0:T(8,128)(2,1)S(1)}, u32[]{:S(2)}, u32[]{:S(2)}) collective-permute-start(bf16[8,128,512]{2,1,0:T(8,128)(2,1)S(1)} %pack.9.refs_6_), channel_id=1, source_target_pairs={{4,8},{6,10},{8,4},{10,6},{5,9},{7,11},{9,5},{11,7},{20,24},{22,26... | collective-permute-start | bytes 3145736 | tf_op jit(solution)/shard_map/ppermute | solution.py:637
  80.4 26.3 %collective-permute-start.10 = (bf16[8,128,512]{2,1,0:T(8,128)(2,1)S(1)}, bf16[8,128,512]{2,1,0:T(8,128)(2,1)S(1)}, u32[]{:S(2)}, u32[]{:S(2)}) collective-permute-start(bf16[8,128,512]{2,1,0:T(8,128)(2,1)S(1)} %get-tuple-element.77), channel_id=1, source_target_pairs={{0,4},{2,6},{4,0},{6,2},{8,12},{10,14},{12,8},{14,10},{1,5},{3,7},... | collective-permute-start | bytes 3145736 | tf_op jit(solution)/shard_map/ppermute | solution.py:637
  83.3 24.9 %collective-permute-start.13 = (bf16[8,128,512]{2,1,0:T(8,128)(2,1)S(1)}, bf16[8,128,512]{2,1,0:T(8,128)(2,1)S(1)}, u32[]{:S(2)}, u32[]{:S(2)}) collective-permute-start(bf16[8,128,512]{2,1,0:T(8,128)(2,1)S(1)} %get-tuple-element.78.refs_9_), channel_id=1, source_target_pairs={{0,2},{2,0},{4,6},{6,4},{8,10},{10,8},{12,14},{14,12},{1,3},{3,1},... | collective-permute-start | bytes 3145736 | tf_op jit(solution)/shard_map/ppermute | solution.py:637
  83.6 0.7 collective-permute-start.12
  111.2 31.2 %collective-permute-start.14 = (bf16[8,128,512]{2,1,0:T(8,128)(2,1)S(1)}, bf16[8,128,512]{2,1,0:T(8,128)(2,1)S(1)}, u32[]{:S(2)}, u32[]{:S(2)}) collective-permute-start(bf16[8,128,512]{2,1,0:T(8,128)(2,1)S(1)} %get-tuple-element.79), channel_id=1, source_target_pairs={{0,4},{2,6},{4,0},{6,2},{8,12},{10,14},{12,8},{14,10},{1,5},{3,7},... | collective-permute-start | bytes 3145736 | tf_op jit(solution)/shard_map/ppermute | solution.py:637
  120.8 20.3 %collective-permute-start.15 = (bf16[7,128,512]{2,1,0:T(8,128)(2,1)S(1)}, bf16[7,128,512]{2,1,0:T(8,128)(2,1)S(1)}, u32[]{:S(2)}, u32[]{:S(2)}) collective-permute-start(bf16[7,128,512]{2,1,0:T(8,128)(2,1)S(1)} %get-tuple-element.80.refs_11_), channel_id=1, source_target_pairs={{0,2},{2,0},{4,6},{6,4},{8,10},{10,8},{12,14},{14,12},{1,3},{3,1},... | collective-permute-start | bytes 2752520 | tf_op jit(solution)/shard_map/ppermute | solution.py:637
  120.8 26.7 %slice-start = ((s8[6291456]{0:T(1024)(128)(4,1)}), s8[4194304]{0:T(1024)(128)(4,1)S(1)}, s32[]{:S(2)}) async-start(s8[6291456]{0:T(1024)(128)(4,1)} %bitcast.23), calls=%async_computation.3 | async-start | bytes 8388608
  120.8 26.7 %copy-start.5 = (bf16[4,128,512]{2,1,0:T(8,128)(2,1)S(1)}, bf16[4,128,512]{2,1,0:T(8,128)(2,1)}, u32[]{:S(2)}) copy-start(bf16[4,128,512]{2,1,0:T(8,128)(2,1)} %copy-done.4) | copy-start | bytes 1572868
  120.8 26.7 %slice-start.1 = ((s8[6291456]{0:T(1024)(128)(4,1)}), s8[2097152]{0:T(1024)(128)(4,1)S(1)}, s32[]{:S(2)}) async-start(s8[6291456]{0:T(1024)(128)(4,1)} %bitcast.23), calls=%async_computation.4 | async-start | bytes 4194304
  120.8 26.7 %copy-start.12 = (s32[32]{0:T(128)S(1)}, s32[32]{0:T(128)}, u32[]{:S(2)}) copy-start(s32[32]{0:T(128)} %get-tuple-element.74.table_ref) | copy-start | bytes 388
  120.8 26.7 %copy-start.18 = (bf16[512,1536]{1,0:T(8,128)(2,1)S(1)}, bf16[512,1536]{1,0:T(8,128)(2,1)}, u32[]{:S(2)}) copy-start(bf16[512,1536]{1,0:T(8,128)(2,1)} %refs_15_.3) | copy-start | bytes 4718596
  120.8 26.7 %copy-start.28 = (bf16[512,512]{1,0:T(8,128)(2,1)S(1)}, bf16[512,512]{1,0:T(8,128)(2,1)}, u32[]{:S(2)}) copy-start(bf16[512,512]{1,0:T(8,128)(2,1)} %refs_16_.1) | copy-start | bytes 1572868
  120.8 0.8 collective-permute-start.16
  146.0 19.9 %collective-permute-start.17 = (bf16[6,128,512]{2,1,0:T(8,128)(2,1)S(1)}, bf16[6,128,512]{2,1,0:T(8,128)(2,1)S(1)}, u32[]{:S(2)}, u32[]{:S(2)}) collective-permute-start(bf16[6,128,512]{2,1,0:T(8,128)(2,1)S(1)} %get-tuple-element.83), channel_id=1, source_target_pairs={{0,4},{2,6},{4,0},{6,2},{8,12},{10,14},{12,8},{14,10},{1,5},{3,7},... | collective-permute-start | bytes 2359304 | tf_op jit(solution)/shard_map/ppermute | solution.py:637
  147.5 18.4 %collective-permute-start.18 = (bf16[6,128,512]{2,1,0:T(8,128)(2,1)S(1)}, bf16[6,128,512]{2,1,0:T(8,128)(2,1)S(1)}, u32[]{:S(2)}, u32[]{:S(2)}) collective-permute-start(bf16[6,128,512]{2,1,0:T(8,128)(2,1)S(1)} %get-tuple-element.81.refs_11_), channel_id=1, source_target_pairs={{0,2},{2,0},{4,6},{6,4},{8,10},{10,8},{12,14},{14,12},{1,3},{3,1},... | collective-permute-start | bytes 2359304 | tf_op jit(solution)/shard_map/ppermute | solution.py:637
  163.6 31.7 %collective-permute-start.20 = (bf16[8,128,512]{2,1,0:T(8,128)(2,1)}, bf16[8,128,512]{2,1,0:T(8,128)(2,1)}, u32[]{:S(2)}, u32[]{:S(2)}) collective-permute-start(bf16[8,128,512]{2,1,0:T(8,128)(2,1)} %get-tuple-element.86), channel_id=1, source_target_pairs={{0,1},{2,3},{4,5},{6,7},{8,9},{10,11},{12,13},{14,15},{16,17},{18,... | collective-permute-start | bytes 3145736 | tf_op jit(solution)/shard_map/ppermute | solution.py:755
  167.0 16.8 %collective-permute-start.19 = (bf16[6,128,512]{2,1,0:T(8,128)(2,1)S(1)}, bf16[6,128,512]{2,1,0:T(8,128)(2,1)S(1)}, u32[]{:S(2)}, u32[]{:S(2)}) collective-permute-start(bf16[6,128,512]{2,1,0:T(8,128)(2,1)S(1)} %pack.13.refs_13_), channel_id=1, source_target_pairs={{0,2},{2,0},{4,6},{6,4},{8,10},{10,8},{12,14},{14,12},{1,3},{3,1},... | collective-permute-start | bytes 2359304 | tf_op jit(solution)/shard_map/ppermute | solution.py:637
  179.0 16.3 %collective-permute-start.21 = (bf16[4,128,512]{2,1,0:T(8,128)(2,1)}, bf16[4,128,512]{2,1,0:T(8,128)(2,1)}, u32[]{:S(2)}, u32[]{:S(2)}) collective-permute-start(bf16[4,128,512]{2,1,0:T(8,128)(2,1)} %get-tuple-element.87), channel_id=1, source_target_pairs={{0,1},{2,3},{4,5},{6,7},{8,9},{10,11},{12,13},{14,15},{16,17},{18,... | collective-permute-start | bytes 1572872 | tf_op jit(solution)/shard_map/ppermute | solution.py:755
  194.0 3.0 %collective-permute-start.22 = (bf16[4,128,512]{2,1,0:T(8,128)(2,1)}, bf16[4,128,512]{2,1,0:T(8,128)(2,1)S(1)}, u32[]{:S(2)}, u32[]{:S(2)}) collective-permute-start(bf16[4,128,512]{2,1,0:T(8,128)(2,1)} %get-tuple-element.88), channel_id=1, source_target_pairs={{0,1},{2,3},{4,5},{6,7},{8,9},{10,11},{12,13},{14,15},{16,17},{18,... | collective-permute-start | bytes 1572872 | tf_op jit(solution)/shard_map/ppermute | solution.py:755
  199.9 21.4 %copy-start.19 = (bf16[512,512]{1,0:T(8,128)(2,1)S(1)}, bf16[512,512]{1,0:T(8,128)(2,1)}, u32[]{:S(2)}) copy-start(bf16[512,512]{1,0:T(8,128)(2,1)} %refs_7_.1) | copy-start | bytes 1572868
  199.9 21.4 %copy-start.24 = (s32[1,16,2]{1,2,0:T(2,128)S(1)}, s32[1,16,2]{1,2,0:T(2,128)}, u32[]{:S(2)}) copy-start(s32[1,16,2]{1,2,0:T(2,128)} %param.13) | copy-start | bytes 388
  216.3 3.0 %collective-permute-start.23 = (f32[2,128]{1,0:T(2,128)S(1)}, f32[2,128]{1,0:T(2,128)S(1)}, u32[]{:S(2)}, u32[]{:S(2)}) collective-permute-start(f32[2,128]{1,0:T(2,128)S(1)} %get-tuple-element.90), channel_id=1, source_target_pairs={{1,0},{3,2},{5,4},{7,6},{9,8},{11,10},{13,12},{15,14},{17,16},{19,... | collective-permute-start | bytes 3080 | tf_op jit(solution)/shard_map/ppermute | solution.py:772
  (16 other events, 93.3 us)
